TPU v7x, 256 devices: a whole 4x4x8 slice. The times are simulated.
256 devices in a mesh: ctx: 64 (over x, y_lo, z), head: 4 (over y_hi, core).
Axes of the slice: x: 4, y: 4 (y_hi: 2, y_lo: 2; y = y_hi * 2 + y_lo), z: 8, core: 2. Of those that a mesh axis runs over, the one named last changes fastest.
Arguments:
- query: bfloat16 [16384, 16, 128], P('ctx', 'head'), may hold values from -24 to 24
- key_proj: bfloat16 [16384, 4, 128], P('ctx', 'head'), may hold values from -24 to 24
- value: bfloat16 [16384, 4, 128], P('ctx', 'head'), may hold values from -6 to 6
- output: bfloat16 [16384, 16, 128], P('ctx', 'head'), may hold values from -6 to 6
- lse: float32 [16384, 16], P('ctx', 'head')
- d_output: bfloat16 [16384, 16, 128], P('ctx', 'head'), may hold values from -6 to 6
- block_order: int32 [128], replicated, may hold values from 0 to 127, as said below
Outputs:
- d_query: float32 [16384, 16, 128], P('ctx', 'head')
- d_key: float32 [16384, 4, 128], P('ctx', 'head')
- d_value: float32 [16384, 4, 128], P('ctx', 'head')
Inputs may be any that keep to these rules, and one draw needn't show every extreme that they name: `block_order`: a permutation of the 128 blocks: for some permutation s of the ctx indices, either every ctx index d holds blocks s(d) and 127 - s(d) in its two slots, or every one holds blocks 2 s(d) and 2 s(d) + 1.
All inputs are finite; a program needn't handle non-finite values.
Results may differ from a plain program's by a relative error of at most 0.008.
Values may be sent and summed in bfloat16 or wider, within the bound.
A program may use at most 64 MiB of HBM per device.

v0:
```python
import jax
import jax.numpy as jnp
from jax import lax
from jax.sharding import PartitionSpec as P


def passed_along(value, axis, steps):
    count = lax.axis_size(axis)
    pairs = [(source, (source + steps) % count) for source in range(count)]
    return lax.ppermute(value, axis, pairs)


def lookup(lookup_table, wanted):
    entries = lookup_table.shape[0]
    hit = wanted[:, None] == jnp.arange(entries, dtype=jnp.int32)[None, :]
    return jnp.sum(jnp.where(hit, lookup_table[None, :], 0), axis=1)


def token_positions(block_order, row_ids, tok_width):
    half_rows = tok_width // 2
    device = row_ids // tok_width
    slot_index = row_ids % tok_width // half_rows
    return lookup(block_order, 2 * device + slot_index) * half_rows + row_ids % half_rows


def blockwise(carried, pieces, first_row, base, half_rows, tile_fn):
    row_count = pieces[0].shape[0]

    def step(step_index, inner):
        offset = step_index * half_rows
        tile_set = tuple(
            (lax.dynamic_slice_in_dim(piece, offset, half_rows, 0) for piece in pieces)
        )
        return tile_fn(inner, tile_set, first_row + offset, base + offset)

    return lax.fori_loop(0, row_count // half_rows, step, carried)


def per_device(query, key_proj, value, output, lse, d_output, block_order):
    tok_width = query.shape[0]
    half_rows = tok_width // 2
    group_size = query.shape[1]
    head_dim = query.shape[2]
    score_scale = head_dim ** (-0.5)
    own_index = lax.axis_index("ctx")
    cycle_size = lax.axis_size("ctx")
    keys = key_proj[:, 0, :]
    values = value[:, 0, :]
    local_rows = own_index * tok_width + jnp.arange(tok_width, dtype=jnp.int32)
    query_pos = token_positions(block_order, local_rows, tok_width)
    delta = jnp.sum(d_output.astype(jnp.float32) * output.astype(jnp.float32), axis=2).T
    log_total = lse.T
    query_parts = [slice(0, half_rows), slice(half_rows, tok_width)]

    def grad_tile(carried, tile_set, first_row, at_row):
        key_tile, value_tile = tile_set
        tile_rows = key_tile.shape[0]
        key_pos = token_positions(
            block_order, first_row + jnp.arange(tile_rows, dtype=jnp.int32), tok_width
        )
        for query_part in query_parts:
            part_pos = query_pos[query_part]

            def live(inner, query_part=query_part, part_pos=part_pos):
                dq_acc, dk_acc, dv_acc = inner
                query_tile = query[query_part]
                grad_tile_out = d_output[query_part]
                scores = score_scale * jnp.einsum(
                    "igd,jd->gij", query_tile, key_tile, preferred_element_type=jnp.float32
                )
                causal = key_pos[None, None, :] <= part_pos[None, :, None]
                shifted = jnp.where(causal, scores - log_total[:, query_part][:, :, None], 0.0)
                probs = jnp.where(causal, jnp.exp(shifted), 0.0)
                probs_low = probs.astype(jnp.bfloat16)
                grad_probs = jnp.einsum(
                    "igd,jd->gij", grad_tile_out, value_tile, preferred_element_type=jnp.float32
                )
                grad_scores = probs * (grad_probs - delta[:, query_part][:, :, None])
                grad_low = grad_scores.astype(jnp.bfloat16)
                dq_acc = dq_acc.at[query_part].add(
                    score_scale
                    * jnp.einsum(
                        "gij,jd->igd", grad_low, key_tile, preferred_element_type=jnp.float32
                    )
                )
                key_term = score_scale * jnp.einsum(
                    "gij,igd->jd", grad_low, query_tile, preferred_element_type=jnp.float32
                )
                value_term = jnp.einsum(
                    "gij,igd->jd", probs_low, grad_tile_out, preferred_element_type=jnp.float32
                )
                dk_acc = lax.dynamic_update_slice_in_dim(
                    dk_acc,
                    lax.dynamic_slice_in_dim(dk_acc, at_row, tile_rows, 0) + key_term,
                    at_row,
                    0,
                )
                dv_acc = lax.dynamic_update_slice_in_dim(
                    dv_acc,
                    lax.dynamic_slice_in_dim(dv_acc, at_row, tile_rows, 0) + value_term,
                    at_row,
                    0,
                )
                return (dq_acc, dk_acc, dv_acc)

            carried = lax.cond(
                jnp.min(key_pos) <= jnp.max(part_pos), live, lambda inner: inner, carried
            )
        return carried

    def visit(dq_acc, key_tile, value_tile, dk_acc, dv_acc, anchor):
        return blockwise(
            (dq_acc, dk_acc, dv_acc),
            (key_tile, value_tile),
            anchor * tok_width,
            0,
            half_rows,
            grad_tile,
        )

    dq_start = jnp.zeros((tok_width, group_size, head_dim), jnp.float32)
    grad_zero = jnp.zeros((tok_width, head_dim), jnp.float32)

    def cycle_step(step_index, carried):
        dq_acc, key_tile, value_tile, dk_acc, dv_acc = carried
        dq_acc, dk_acc, dv_acc = visit(
            dq_acc, key_tile, value_tile, dk_acc, dv_acc, (own_index - step_index) % cycle_size
        )
        key_tile, value_tile = passed_along((key_tile, value_tile), "ctx", 1)
        dk_acc, dv_acc = passed_along((dk_acc, dv_acc), "ctx", 1)
        return (dq_acc, key_tile, value_tile, dk_acc, dv_acc)

    dq_acc, key_tile, value_tile, dk_acc, dv_acc = lax.fori_loop(
        0, cycle_size, cycle_step, (dq_start, keys, values, grad_zero, grad_zero)
    )
    return (dq_acc, dk_acc[:, None, :], dv_acc[:, None, :])


def solution(mesh):
    in_specs = (
        P("ctx", "head", None),
        P("ctx", "head", None),
        P("ctx", "head", None),
        P("ctx", "head", None),
        P("ctx", "head"),
        P("ctx", "head", None),
        P(),
    )
    out_specs = (P("ctx", "head", None), P("ctx", "head", None), P("ctx", "head", None))
    return jax.shard_map(
        per_device, mesh=mesh, in_specs=in_specs, out_specs=out_specs, check_vma=False
    )
```

profile of v0, /device:TPU:16, one launch (start us, length us, event | category | flops | bytes accessed | tf_op | source)
XLA Modules:
  0.0 1455.7 jit_solution(3509846755834878117)
XLA Ops:
  5.5 1449.1 %while.80 = (s32[]{:T(128)}, f32[256,4,128]{2,0,1:T(8,128)S(1)}, bf16[256,128]{1,0:T(8,128)(2,1)S(1)}, bf16[256,128]{1,0:T(8,128)(2,1)S(1)}, f32[256,128]{1,0:T(...) while((s32[]{:T(128)}, f32[256,4,128]{2,0,1:T(8,128)S(1)}, ...), condition=%wide.region_13.14_spmd, body=%wide.region_4.0_spmd.sunk | while | flops 169269648 | bytes 7766313 | solution.py:133
  5.5 10.7 while.81
  58.3 9.5 while.81
  68.2 10.4 collective-permute-done.2
  81.5 9.5 while.81
  91.4 9.6 collective-permute-done.2
  103.8 9.5 while.81
  125.5 9.5 while.81
  233.6 9.5 while.81
  276.8 9.5 while.81
  320.0 9.5 while.81
  341.7 9.5 while.81
  364.0 9.5 while.81
  412.1 9.5 while.81
  422.0 10.2 collective-permute-done.2
  437.8 9.5 while.81
  447.7 10.3 collective-permute-done.2
  472.6 10.4 collective-permute-done.2
  496.8 10.4 collective-permute-done.2
  510.1 9.5 while.81
  520.0 9.5 collective-permute-done.2
  532.3 9.5 while.81
  554.0 9.5 while.81
  618.8 9.5 while.81
  683.7 9.5 while.81
  770.2 9.5 while.81
  792.6 9.5 while.81
  840.7 9.5 while.81
  850.6 10.2 collective-permute-done.2
  876.4 10.3 collective-permute-done.2
  891.5 9.5 while.81
  901.3 10.4 collective-permute-done.2
  925.5 10.4 collective-permute-done.2
  948.6 9.6 collective-permute-done.2
  961.0 9.5 while.81
  982.6 9.5 while.81
  1047.5 9.5 while.81
  1090.7 9.5 while.81
  1112.4 9.5 while.81
  1244.7 9.5 while.81
  1269.3 9.5 while.81
  1279.2 10.2 collective-permute-done.2
  1304.9 10.3 collective-permute-done.2
  1320.0 9.5 while.81
  1329.9 10.4 collective-permute-done.2
  1354.1 10.4 collective-permute-done.2
  1367.4 9.5 while.81
  1377.3 9.6 collective-permute-done.2
  (2831 shorter events, 1405.4 us)
Async XLA Ops:
  16.2 13.2 collective-permute-start.2
  18.2 14.0 collective-permute-start.3
  20.1 13.3 collective-permute-start
  43.8 13.1 collective-permute-start.3
  43.9 13.7 collective-permute-start
  44.0 14.3 collective-permute-start.1
  68.0 12.8 collective-permute-start
  68.1 13.4 collective-permute-start.1
  373.8 13.6 collective-permute-start.1
  397.2 13.4 collective-permute-start
  397.3 14.7 %collective-permute-start.1 = (bf16[256,128]{1,0:T(8,128)(2,1)S(1)}, bf16[256,128]{1,0:T(8,128)(2,1)S(1)}, u32[]{:S(2)}, u32[]{:S(2)}) collective-permute-start(bf16[256,128]{1,0:T(8,128)(2,1)S(1)} %get-tuple-element.1501), channel_id=1, source_target_pairs={{0,4},{4,8},{8,12},{12,16},{16,20},{20,24},{24,28},{28,32},{32,36}... | collective-permute-start | bytes 196616 | tf_op jit(solution)/shard_map/while/body/eval_jaxpr/ppermute | solution.py:10
  421.7 13.3 collective-permute-start.3
  421.8 14.6 %collective-permute-start = (bf16[256,128]{1,0:T(8,128)(2,1)S(1)}, bf16[256,128]{1,0:T(8,128)(2,1)S(1)}, u32[]{:S(2)}, u32[]{:S(2)}) collective-permute-start(bf16[256,128]{1,0:T(8,128)(2,1)S(1)} %get-tuple-element.1503), channel_id=1, source_target_pairs={{0,4},{4,8},{8,12},{12,16},{16,20},{20,24},{24,28},{28,32},{32,36}... | collective-permute-start | bytes 196616 | tf_op jit(solution)/shard_map/while/body/eval_jaxpr/ppermute | solution.py:10
  421.9 15.9 %collective-permute-start.1 = (bf16[256,128]{1,0:T(8,128)(2,1)S(1)}, bf16[256,128]{1,0:T(8,128)(2,1)S(1)}, u32[]{:S(2)}, u32[]{:S(2)}) collective-permute-start(bf16[256,128]{1,0:T(8,128)(2,1)S(1)} %get-tuple-element.1501), channel_id=1, source_target_pairs={{0,4},{4,8},{8,12},{12,16},{16,20},{20,24},{24,28},{28,32},{32,36}... | collective-permute-start | bytes 196616 | tf_op jit(solution)/shard_map/while/body/eval_jaxpr/ppermute | solution.py:10
  447.4 13.4 collective-permute-start.3
  447.5 14.5 collective-permute-start
  447.6 15.2 %collective-permute-start.1 = (bf16[256,128]{1,0:T(8,128)(2,1)S(1)}, bf16[256,128]{1,0:T(8,128)(2,1)S(1)}, u32[]{:S(2)}, u32[]{:S(2)}) collective-permute-start(bf16[256,128]{1,0:T(8,128)(2,1)S(1)} %get-tuple-element.1501), channel_id=1, source_target_pairs={{0,4},{4,8},{8,12},{12,16},{16,20},{20,24},{24,28},{28,32},{32,36}... | collective-permute-start | bytes 196616 | tf_op jit(solution)/shard_map/while/body/eval_jaxpr/ppermute | solution.py:10
  472.4 13.1 collective-permute-start.3
  472.5 13.7 collective-permute-start
  472.6 14.3 collective-permute-start.1
  496.7 13.4 collective-permute-start.1
  802.4 13.7 collective-permute-start.1
  825.8 13.5 collective-permute-start
  825.9 14.8 %collective-permute-start.1 = (bf16[256,128]{1,0:T(8,128)(2,1)S(1)}, bf16[256,128]{1,0:T(8,128)(2,1)S(1)}, u32[]{:S(2)}, u32[]{:S(2)}) collective-permute-start(bf16[256,128]{1,0:T(8,128)(2,1)S(1)} %get-tuple-element.1501), channel_id=1, source_target_pairs={{0,4},{4,8},{8,12},{12,16},{16,20},{20,24},{24,28},{28,32},{32,36}... | collective-permute-start | bytes 196616 | tf_op jit(solution)/shard_map/while/body/eval_jaxpr/ppermute | solution.py:10
  850.3 13.3 collective-permute-start.3
  850.4 14.6 %collective-permute-start = (bf16[256,128]{1,0:T(8,128)(2,1)S(1)}, bf16[256,128]{1,0:T(8,128)(2,1)S(1)}, u32[]{:S(2)}, u32[]{:S(2)}) collective-permute-start(bf16[256,128]{1,0:T(8,128)(2,1)S(1)} %get-tuple-element.1503), channel_id=1, source_target_pairs={{0,4},{4,8},{8,12},{12,16},{16,20},{20,24},{24,28},{28,32},{32,36}... | collective-permute-start | bytes 196616 | tf_op jit(solution)/shard_map/while/body/eval_jaxpr/ppermute | solution.py:10
  850.5 15.9 %collective-permute-start.1 = (bf16[256,128]{1,0:T(8,128)(2,1)S(1)}, bf16[256,128]{1,0:T(8,128)(2,1)S(1)}, u32[]{:S(2)}, u32[]{:S(2)}) collective-permute-start(bf16[256,128]{1,0:T(8,128)(2,1)S(1)} %get-tuple-element.1501), channel_id=1, source_target_pairs={{0,4},{4,8},{8,12},{12,16},{16,20},{20,24},{24,28},{28,32},{32,36}... | collective-permute-start | bytes 196616 | tf_op jit(solution)/shard_map/while/body/eval_jaxpr/ppermute | solution.py:10
  876.1 13.4 collective-permute-start.3
  876.2 14.6 collective-permute-start
  876.3 15.2 %collective-permute-start.1 = (bf16[256,128]{1,0:T(8,128)(2,1)S(1)}, bf16[256,128]{1,0:T(8,128)(2,1)S(1)}, u32[]{:S(2)}, u32[]{:S(2)}) collective-permute-start(bf16[256,128]{1,0:T(8,128)(2,1)S(1)} %get-tuple-element.1501), channel_id=1, source_target_pairs={{0,4},{4,8},{8,12},{12,16},{16,20},{20,24},{24,28},{28,32},{32,36}... | collective-permute-start | bytes 196616 | tf_op jit(solution)/shard_map/while/body/eval_jaxpr/ppermute | solution.py:10
  901.1 13.1 collective-permute-start.3
  901.2 13.7 collective-permute-start
  901.2 14.3 collective-permute-start.1
  925.4 13.4 collective-permute-start.1
  1231.0 13.6 collective-permute-start.1
  1254.4 13.5 collective-permute-start
  1254.5 14.8 %collective-permute-start.1 = (bf16[256,128]{1,0:T(8,128)(2,1)S(1)}, bf16[256,128]{1,0:T(8,128)(2,1)S(1)}, u32[]{:S(2)}, u32[]{:S(2)}) collective-permute-start(bf16[256,128]{1,0:T(8,128)(2,1)S(1)} %get-tuple-element.1501), channel_id=1, source_target_pairs={{0,4},{4,8},{8,12},{12,16},{16,20},{20,24},{24,28},{28,32},{32,36}... | collective-permute-start | bytes 196616 | tf_op jit(solution)/shard_map/while/body/eval_jaxpr/ppermute | solution.py:10
  1278.9 13.3 collective-permute-start.3
  1279.0 14.6 %collective-permute-start = (bf16[256,128]{1,0:T(8,128)(2,1)S(1)}, bf16[256,128]{1,0:T(8,128)(2,1)S(1)}, u32[]{:S(2)}, u32[]{:S(2)}) collective-permute-start(bf16[256,128]{1,0:T(8,128)(2,1)S(1)} %get-tuple-element.1503), channel_id=1, source_target_pairs={{0,4},{4,8},{8,12},{12,16},{16,20},{20,24},{24,28},{28,32},{32,36}... | collective-permute-start | bytes 196616 | tf_op jit(solution)/shard_map/while/body/eval_jaxpr/ppermute | solution.py:10
  1279.1 15.9 %collective-permute-start.1 = (bf16[256,128]{1,0:T(8,128)(2,1)S(1)}, bf16[256,128]{1,0:T(8,128)(2,1)S(1)}, u32[]{:S(2)}, u32[]{:S(2)}) collective-permute-start(bf16[256,128]{1,0:T(8,128)(2,1)S(1)} %get-tuple-element.1501), channel_id=1, source_target_pairs={{0,4},{4,8},{8,12},{12,16},{16,20},{20,24},{24,28},{28,32},{32,36}... | collective-permute-start | bytes 196616 | tf_op jit(solution)/shard_map/while/body/eval_jaxpr/ppermute | solution.py:10
  1304.7 13.4 collective-permute-start.3
  1304.8 14.6 %collective-permute-start = (bf16[256,128]{1,0:T(8,128)(2,1)S(1)}, bf16[256,128]{1,0:T(8,128)(2,1)S(1)}, u32[]{:S(2)}, u32[]{:S(2)}) collective-permute-start(bf16[256,128]{1,0:T(8,128)(2,1)S(1)} %get-tuple-element.1503), channel_id=1, source_target_pairs={{0,4},{4,8},{8,12},{12,16},{16,20},{20,24},{24,28},{28,32},{32,36}... | collective-permute-start | bytes 196616 | tf_op jit(solution)/shard_map/while/body/eval_jaxpr/ppermute | solution.py:10
  1304.8 15.2 %collective-permute-start.1 = (bf16[256,128]{1,0:T(8,128)(2,1)S(1)}, bf16[256,128]{1,0:T(8,128)(2,1)S(1)}, u32[]{:S(2)}, u32[]{:S(2)}) collective-permute-start(bf16[256,128]{1,0:T(8,128)(2,1)S(1)} %get-tuple-element.1501), channel_id=1, source_target_pairs={{0,4},{4,8},{8,12},{12,16},{16,20},{20,24},{24,28},{28,32},{32,36}... | collective-permute-start | bytes 196616 | tf_op jit(solution)/shard_map/while/body/eval_jaxpr/ppermute | solution.py:10
  1329.7 13.1 collective-permute-start.3
  1329.7 13.7 collective-permute-start
  1329.8 14.3 collective-permute-start.1
  1353.9 12.8 collective-permute-start
  1354.0 13.4 collective-permute-start.1
  (217 other events, 2262.4 us)
where the time goes:
time: 1460 us
  waiting for transfers between devices  800 us (55%)
  loops' own time  355 us (24%)
  other arithmetic  129 us (9%)
  matrix products  129 us (9%)
  starting transfers between devices  32.6 us (2%)
    ppermute x256, waiting for transfers between devices, passed_along(): return lax.ppermute(value, axis, pairs)  800 us
    another operation x64, loops' own time, blockwise(): return lax.fori_loop(0, row_count // half_rows, step, carried)  338 us
    reduce_min x128, other arithmetic, grad_tile(): jnp.min(key_pos) <= jnp.max(part_pos)  92.3 us
    ppermute x256, starting transfers between devices, passed_along(): return lax.ppermute(value, axis, pairs)  32.6 us
    dot_general x129, matrix products, live(): jnp.einsum('gij,jd->igd', grad_low, key_tile, preferred_element_type=jnp....  30.5 us
  transfers between devices with their start and end apart: 256, of which 256 were waited for; matrix products, arithmetic and copies ran while one was open for 0% of the time, Pallas kernels for 0%

commit v1 on v0

v1 whole, which is shorter than its diff:
```python
import functools

import jax
import jax.numpy as jnp
from jax import lax
from jax.experimental import pallas as pl
from jax.experimental.pallas import tpu as pltpu
from jax.sharding import PartitionSpec as P

MESH = pl.DeviceIdType.MESH
LOG2E = 1.4426950408889634
F32 = jnp.float32
BF16 = jnp.bfloat16
BLK = 128
TOK = 256
ROWS = 512
SCALE = BLK ** (-0.5)
NX, NY, NZ = 4, 2, 8
OWN, LEFT, RIGHT, OPP = range(4)


def dot(a, b):
    return lax.dot_general(a, b, (((1,), (0,)), ((), ())), preferred_element_type=F32)


def tile_grads(q, do, qt, dot_t, lse2, delta, k, v, kt, keep=None):
    e = dot(k, qt) * (SCALE * LOG2E) - lse2
    if keep is not None:
        e = jnp.where(keep, e, -jnp.inf)
    p = jnp.exp2(e)
    ds = (p * (dot(v, dot_t) - delta)).astype(BF16)
    return dot(kt, ds), dot(ds, q), dot(p.astype(BF16), do)


def kernel(
    fold, order, q_in, do_in, out_in, lse_in, k_in, v_in, dq_out, dk_out, dv_out,
    qd0, qd1, qd2, qd3, qt0, qt1, qt2, qt3, rw0, rw1, rw2, rw3,
    kv, kt, dqa, dka, ktx, kup, kdn, ytx, yrx, qtx, qrx, orx, ssem, rsem,
):
    ctx = lax.axis_index("ctx")
    x, plane = ctx // (NY * NZ), ctx % (NY * NZ)
    y, z = plane // NZ, plane % NZ
    right = (x + 1) % NX * (NY * NZ) + plane
    left = (x + NX - 1) % NX * (NY * NZ) + plane
    opp = (x + 2) % NX * (NY * NZ) + plane
    partner = x * (NY * NZ) + (1 - y) * NZ + z
    up = ctx - z + (z + 1) % NZ
    down = ctx - z + (z + NZ - 1) % NZ
    qds, qts, rws = (qd0, qd1, qd2, qd3), (qt0, qt1, qt2, qt3), (rw0, rw1, rw2, rw3)
    owners = (ctx, left, right, opp)
    used = []

    def send(src, dst, device):
        index = len(used)
        used.append(index)
        copy = pltpu.make_async_remote_copy(
            src_ref=src, dst_ref=dst, send_sem=ssem.at[index], recv_sem=rsem.at[index],
            device_id={"ctx": device}, device_id_type=MESH,
        )
        return copy

    def begin(*copies):
        for copy in copies:
            copy.start()

    def arrive(*copies):
        for copy in copies:
            copy.wait_recv()

    to_right = [send(qd0.at[j], qd1.at[j], right) for j in range(2)]
    to_right += [send(rw0, rw1, right)]
    to_left = [send(qd0.at[j], qd2.at[j], left) for j in range(2)]
    to_left += [send(rw0, rw2, left)]
    far_right = [send(qd1.at[0], qd3.at[0], right), send(rw1.at[0], rw3.at[0], right)]
    far_left = [send(qd2.at[1], qd3.at[1], left), send(rw2.at[1], rw3.at[1], left)]
    across = send(kv.at[0, 0], kv.at[0, 1], partner)
    up_kv = [[send(kv.at[0, j], kv.at[7, j], up) for j in range(2)]]
    up_kv += [[send(kv.at[8 - s], kv.at[7 - s], up)] for s in (1, 2)] + [[send(kv.at[5, 0], kv.at[4, 0], up)]]
    down_kv = [[send(kv.at[0, j], kv.at[1, j], down) for j in range(2)]]
    down_kv += [[send(kv.at[s], kv.at[s + 1], down)] for s in (1, 2)] + [[send(kv.at[3, 1], kv.at[4, 1], down)]]
    up_sum = {4: send(ktx.at[4, 0], kup.at[3, 0], up)}
    up_sum.update({o: send(ktx.at[o], kup.at[o - 1], up) for o in (3, 2, 1)})
    down_sum = {4: send(ktx.at[4, 1], kdn.at[3, 1], down)}
    down_sum.update({o: send(ktx.at[8 - o], kdn.at[o - 1], down) for o in (3, 2, 1)})
    across_sum = send(ytx, yrx, partner)
    opp_sum = [send(qtx.at[OPP, 0], orx.at[0], right), send(qtx.at[OPP, 1], orx.at[1], left)]
    right_sum = [send(qtx.at[RIGHT, j], qrx.at[0, j], right) for j in (1, 0)]
    left_sum = [send(qtx.at[LEFT, j], qrx.at[1, j], left) for j in (0, 1)]

    kv[0, 0, 0] = k_in[...]
    kv[0, 0, 1] = v_in[...]
    for j in range(2):
        qd0[j, 0] = q_in[j]
        qd0[j, 1] = do_in[j]
        product = do_in[j].astype(F32) * out_in[j].astype(F32)
        rw0[j, 0] = lse_in[j] * LOG2E
        rw0[j, 1] = jnp.sum(product.T, axis=0, keepdims=True)

    barrier = pltpu.get_barrier_semaphore()
    for device in (right, left, partner, up, down):
        pl.semaphore_signal(barrier, inc=1, device_id={"ctx": device}, device_id_type=MESH)
    pl.semaphore_wait(barrier, 5)

    begin(across, up_kv[0][0], down_kv[0][0])
    begin(to_right[0], to_left[1], to_right[2], to_left[2], to_right[1], to_left[0])

    def turn_queries(i):
        for j in range(2):
            for part in range(2):
                qts[i][j, part] = qds[i][j, part].T

    def turn_keys(o):
        for j in range(2):
            kt[o, j] = kv[o, j, 0].T

    turn_queries(OWN)
    kt[0, 0] = kv[0, 0, 0].T
    dqa[...] = jnp.zeros_like(dqa)
    dka[...] = jnp.zeros_like(dka)

    def query_side(i, j):
        return qds[i][j, 0], qds[i][j, 1], qts[i][j, 0], qts[i][j, 1]

    for j in range(2):
        keys = BLK * (j + 1)
        shape = (keys, ROWS)
        keep = lax.broadcasted_iota(jnp.int32, shape, 0) <= (
            lax.broadcasted_iota(jnp.int32, shape, 1) // 4 + j * BLK
        )
        dqt, dk, dv = tile_grads(
            *query_side(OWN, j), rw0[j, 0], rw0[j, 1],
            kv[0, 0, 0, :keys], kv[0, 0, 1, :keys], kt[0, 0, :, :keys], keep,
        )
        dqa[OWN, j] += dqt
        dka[0, 0, 0, :keys] += dk
        dka[0, 0, 1, :keys] += dv

    def first_block(i, o, j):
        owner = x * (NY * NZ) + (y + j) % NY * NZ + (z + o) % NZ
        return order[2 * owners[i]], order[2 * owner]

    def folded(i, o, parts):
        lo = [kv[o, j, :, :BLK] for j in parts]
        dqt, dk, dv = tile_grads(
            *query_side(i, 1), rws[i][1, 0], rws[i][1, 1],
            jnp.concatenate([part[0] for part in lo], axis=0),
            jnp.concatenate([part[1] for part in lo], axis=0),
            jnp.concatenate([kt[o, j, :, :BLK] for j in parts], axis=1),
        )
        early = jnp.zeros((BLK, ROWS), F32)
        for n, j in enumerate(parts):
            query_first, key_first = first_block(i, o, j)
            later = query_first < key_first
            slot = later.astype(jnp.int32)
            weight = later.astype(F32)
            dqb, dkb, dvb = tile_grads(
                *query_side(i, slot), rws[i][slot, 0], rws[i][slot, 1],
                lax.select(later, kv[o, j, 0, BLK:], kv[o, j, 0, :BLK]),
                lax.select(later, kv[o, j, 1, BLK:], kv[o, j, 1, :BLK]),
                lax.select(later, kt[o, j, :, BLK:], kt[o, j, :, :BLK]),
            )
            dqt = dqt + weight * dqb
            early = early + (1.0 - weight) * dqb
            rows = slice(n * BLK, n * BLK + BLK)
            dka[o, j, 0, :BLK] += dk[rows] + (1.0 - weight) * dkb
            dka[o, j, 1, :BLK] += dv[rows] + (1.0 - weight) * dvb
            dka[o, j, 0, BLK:] += weight * dkb
            dka[o, j, 1, BLK:] += weight * dvb
        dqa[i, 0] += early
        dqa[i, 1] += dqt

    def whole(i, o, parts):
        for j in parts:
            query_first, key_first = first_block(i, o, j)
            hidden = jnp.where(query_first > key_first, 0.0, 1e30).astype(F32)
            for slot in range(2):
                dqt, dk, dv = tile_grads(
                    *query_side(i, slot), rws[i][slot, 0] + hidden, rws[i][slot, 1],
                    kv[o, j, 0], kv[o, j, 1], kt[o, j],
                )
                dqa[i, slot] += dqt
                dka[o, j, 0] += dk
                dka[o, j, 1] += dv

    work = folded if fold else whole

    arrive(across)
    begin(up_kv[0][1], down_kv[0][1])
    kt[0, 1] = kv[0, 1, 0].T
    work(OWN, 0, (1,))

    def near(s, carry):
        for hop in (1, 2):
            @pl.when(s == hop)
            def _():
                arrive(*up_kv[hop - 1], *down_kv[hop - 1])
                begin(*up_kv[hop], *down_kv[hop])

        def side(t, carry):
            o = s + t * (NZ - 2 * s)
            turn_keys(o)
            work(OWN, o, (0, 1))
            return carry

        return lax.fori_loop(0, 2, side, carry)

    lax.fori_loop(1, 3, near, jnp.int32(0))

    arrive(to_right[0], to_right[2], to_left[1], to_left[2])
    begin(*far_right, *far_left)
    arrive(to_right[1], to_left[0])
    turn_queries(LEFT)
    turn_queries(RIGHT)

    def sides(t, carry):
        @pl.when(t == 2)
        def _():
            arrive(*up_kv[2], *down_kv[2])
            begin(*up_kv[3], *down_kv[3])

        s = 1 + t // 2
        o = s + t % 2 * (NZ - 2 * s)
        work(LEFT, o, (0, 1))
        work(RIGHT, o, (0, 1))
        return carry

    lax.fori_loop(0, 4, sides, jnp.int32(0))

    arrive(*far_right, *far_left)
    turn_queries(OPP)
    arrive(*up_kv[3], *down_kv[3])
    turn_keys(4)
    turn_keys(3)
    turn_keys(5)

    def last(t, carry):
        s = 4 - (t + 1) // 2
        o = s + (1 - t % 2) * (NZ - 2 * s)

        @pl.when(t < 3)
        def _():
            work(OWN, o, (0, 1))
            work(LEFT, o, (0, 1))
            work(RIGHT, o, (0, 1))

        work(OPP, o, (0, 1))

        @pl.when(t == 0)
        def _():
            ktx[4] = dka[4].astype(BF16)
            begin(up_sum[4], down_sum[4])

        @pl.when(t == 1)
        def _():
            ktx[3, 1] = dka[3, 1].astype(BF16)
            arrive(up_sum[4])
            ktx[3, 0] = (dka[3, 0] + kup[3, 0].astype(F32)).astype(BF16)
            begin(up_sum[3])

        @pl.when(t == 2)
        def _():
            ktx[5, 0] = dka[5, 0].astype(BF16)
            arrive(down_sum[4])
            ktx[5, 1] = (dka[5, 1] + kdn[3, 1].astype(F32)).astype(BF16)
            begin(down_sum[3])

        for hop in (2, 1):
            @pl.when(t == 7 - 2 * hop)
            def _():
                arrive(up_sum[hop + 1])
                ktx[hop] = (dka[hop] + kup[hop].astype(F32)).astype(BF16)
                begin(up_sum[hop])

            @pl.when(t == 8 - 2 * hop)
            def _():
                arrive(down_sum[hop + 1])
                ktx[8 - hop] = (dka[8 - hop] + kdn[hop].astype(F32)).astype(BF16)
                begin(down_sum[hop])

        return carry

    lax.fori_loop(0, 7, last, jnp.int32(0))
    work(OPP, 0, (0, 1))
    qtx[OPP] = dqa[OPP].astype(BF16)
    begin(*opp_sum)
    work(LEFT, 0, (0, 1))
    work(RIGHT, 0, (0, 1))

    qtx[RIGHT, 1] = dqa[RIGHT, 1].astype(BF16)
    qtx[LEFT, 0] = dqa[LEFT, 0].astype(BF16)
    begin(right_sum[0], left_sum[0])
    arrive(*opp_sum)
    qtx[RIGHT, 0] = (dqa[RIGHT, 0] + orx[0].astype(F32)).astype(BF16)
    qtx[LEFT, 1] = (dqa[LEFT, 1] + orx[1].astype(F32)).astype(BF16)
    begin(right_sum[1], left_sum[1])
    arrive(up_sum[1], down_sum[1])
    ytx[...] = (dka[0, 1] + kup[0, 1].astype(F32) + kdn[0, 1].astype(F32)).astype(BF16)
    begin(across_sum)
    total = dka[0, 0] + kup[0, 0].astype(F32) + kdn[0, 0].astype(F32)
    arrive(across_sum)
    total = total + yrx[...].astype(F32)
    dk_out[...] = total[0] * SCALE
    dv_out[...] = total[1]
    for j, (a, b) in enumerate(((1, 0), (0, 1))):
        arrive(right_sum[a], left_sum[b])
        dq = dqa[OWN, j] + qrx[0, j].astype(F32) + qrx[1, j].astype(F32)
        dq_out[j] = dq.T * SCALE

    for copy in to_right + to_left + far_right + far_left + [across, across_sum]:
        copy.wait_send()
    for group in up_kv + down_kv:
        for copy in group:
            copy.wait_send()
    for copy in list(up_sum.values()) + list(down_sum.values()) + opp_sum + right_sum + left_sum:
        copy.wait_send()


N_COPIES = 3 + 3 + 2 + 2 + 1 + 5 + 5 + 4 + 4 + 1 + 2 + 2 + 2


def grads(fold, order, q, do, out, lse, k, v):
    smem = pl.BlockSpec(memory_space=pltpu.SMEM)
    vmem = pl.BlockSpec(memory_space=pltpu.VMEM)
    queries = [pltpu.VMEM((2, 2, ROWS, BLK), BF16)] * 4
    turned = [pltpu.VMEM((2, 2, BLK, ROWS), BF16)] * 4
    rows = [pltpu.VMEM((2, 2, 1, ROWS), F32)] * 4
    return pl.pallas_call(
        functools.partial(kernel, fold),
        out_shape=(
            jax.ShapeDtypeStruct((2, ROWS, BLK), F32),
            jax.ShapeDtypeStruct((TOK, BLK), F32),
            jax.ShapeDtypeStruct((TOK, BLK), F32),
        ),
        in_specs=[smem] + [vmem] * 6,
        out_specs=(vmem, vmem, vmem),
        scratch_shapes=queries + turned + rows + [
            pltpu.VMEM((NZ, NY, 2, TOK, BLK), BF16),
            pltpu.VMEM((NZ, NY, BLK, TOK), BF16),
            pltpu.VMEM((4, 2, BLK, ROWS), F32),
            pltpu.VMEM((NZ, NY, 2, TOK, BLK), F32),
            pltpu.VMEM((NZ, NY, 2, TOK, BLK), BF16),
            pltpu.VMEM((4, NY, 2, TOK, BLK), BF16),
            pltpu.VMEM((4, NY, 2, TOK, BLK), BF16),
            pltpu.VMEM((2, TOK, BLK), BF16),
            pltpu.VMEM((2, TOK, BLK), BF16),
            pltpu.VMEM((4, 2, BLK, ROWS), BF16),
            pltpu.VMEM((2, 2, BLK, ROWS), BF16),
            pltpu.VMEM((2, BLK, ROWS), BF16),
            pltpu.SemaphoreType.DMA((N_COPIES,)),
            pltpu.SemaphoreType.DMA((N_COPIES,)),
        ],
        compiler_params=pltpu.CompilerParams(
            collective_id=0 if fold else 1, has_side_effects=True, vmem_limit_bytes=48 * 1024 * 1024
        ),
        name="folded" if fold else "whole",
    )(order, q, do, out, lse, k, v)


def per_device(query, key_proj, value, output, lse, d_output, block_order):
    args = (
        block_order,
        query.reshape(2, ROWS, BLK),
        d_output.reshape(2, ROWS, BLK),
        output.reshape(2, ROWS, BLK),
        lse.reshape(2, 1, ROWS),
        key_proj.reshape(TOK, BLK),
        value.reshape(TOK, BLK),
    )
    is_folded = block_order[0] + block_order[1] == 2 * NX * NY * NZ - 1
    dq, dk, dv = lax.cond(is_folded, functools.partial(grads, True), functools.partial(grads, False), *args)
    return dq.reshape(query.shape), dk.reshape(key_proj.shape), dv.reshape(value.shape)


def solution(mesh):
    in_specs = (
        P("ctx", "head", None),
        P("ctx", "head", None),
        P("ctx", "head", None),
        P("ctx", "head", None),
        P("ctx", "head"),
        P("ctx", "head", None),
        P(),
    )
    out_specs = (P("ctx", "head", None), P("ctx", "head", None), P("ctx", "head", None))
    return jax.shard_map(
        per_device, mesh=mesh, in_specs=in_specs, out_specs=out_specs, check_vma=False
    )
```

time: 1460 us -> 101 us (0.07)
  waiting for transfers between devices: 800 us -> 0 us
  loops' own time: 355 us -> 0.27 us
  matrix products: 129 us -> 0 us
  other arithmetic: 129 us -> 0 us
  Pallas kernels: 0 us -> 92.2 us
  starting transfers between devices: 32.6 us -> 0 us
    ppermute x256 -> x0, waiting for transfers between devices: 800 us -> none  [passed_along(): return lax.ppermute(value, axis, pairs)]
    another operation x321 -> x1, loops' own time: 355 us -> 0.27 us  [per_device(): lax.cond(is_folded, functools.partial(grads, True), functools.partial(gra...]
    dot_general x645 -> x0, matrix products: 129 us -> none  [the longest x129 30.5 us: live(): jnp.einsum('gij,jd->igd', grad_low, key_tile, preferred_element_type=jnp....]
    reduce_min x128 -> x0, other arithmetic: 92.3 us -> none  [grad_tile(): jnp.min(key_pos) <= jnp.max(part_pos)]
    pallas_call x0 -> x1, Pallas kernels: none -> 92.2 us  [grads(): pl.pallas_call(functools.partial(kernel, fold), out_shape=(jax.ShapeDtype...]
    ppermute x256 -> x0, starting transfers between devices: 32.6 us -> none  [passed_along(): return lax.ppermute(value, axis, pairs)]
    reduce_sum x130 -> x0, other arithmetic: 22.3 us -> none  [the longest x129 21.9 us: lookup(): return jnp.sum(jnp.where(hit, lookup_table[None, :], 0), axis=1)]
  transfers between devices with their start and end apart: 256 -> 0, of which waited for: 256 -> 0; matrix products, arithmetic and copies ran while one was open for 0% -> 0% of each run, Pallas kernels for 0% -> 0%
where the time goes in v1:
time: 101 us; the launch traced here: 99.3 us
  Pallas kernels  92.2 us (91%)
  local copies, waits for them, and re-layouts  4.89 us (5%)
  between operations  1.97 us (2%)
    pallas_call x1, Pallas kernels, grads(): pl.pallas_call(functools.partial(kernel, fold), out_shape=(jax.ShapeDtype...  92.2 us
    unnamed x8, local copies, waits for them, and re-layouts  3.45 us

profile of v1, /device:TPU:16, one launch (start us, length us, event | category | flops | bytes accessed | tf_op | source)
XLA Modules:
  0.0 99.3 jit_solution(15619969697267367565)
XLA Ops:
  0.6 0.0 copy-start
  0.6 1.3 %fusion = (s32[1]{0:T(128)}, s32[1]{0:T(128)}) fusion(s32[128]{0:T(128)} %param.15), kind=kLoop, calls=%fused_computation | loop fusion | bytes 16 | tf_op jit(solution)/shard_map/slice | solution.py:369
  3.3 0.8 copy.11
  4.1 0.0 copy-start.1
  4.1 0.1 reshape.53
  4.2 0.0 copy-done
  4.2 0.5 copy-done.1
  4.7 92.5 %conditional.1 = ((f32[2,512,128]{2,1,0:T(8,128)S(1)}, f32[256,128]{1,0:T(8,128)S(1)}, f32[256,128]{1,0:T(8,128)S(1)})) conditional(s32[]{:T(128)} %bitcast, (s32[128]{0:T(128)S(1)}, bf16[2,512,128]{2,1,0:T(8,128)(2,1)S(1)}, bf16[2,512,128]{2,1,0:T(8,128)(2,1)}, bf16[2,512,128]{2,1,0:T(8,128)(2,1)}, f32[2,1,512]{2,0,1:T(2,128)S(1)}, ...), branch_computations={%region_0.0_spmd, %region_1.0_spmd} | conditional | bytes 8200 | solution.py:370
  4.7 92.2 %whole.1 = (f32[2,512,128]{2,1,0:T(8,128)S(1)}, f32[256,128]{1,0:T(8,128)S(1)}, f32[256,128]{1,0:T(8,128)S(1)}) custom-call(s32[128]{0:T(128)S(1)} %get-tuple-element.37.order, bf16[2,512,128]{2,1,0:T(8,128)(2,1)S(1)} %get-tuple-element.38.q_in, bf16[2,512,128]{2,1,0:T(8,128)(2,1)} %get-tuple-element.39.do_in, ...), custom_call_target="tpu_custom_call" | custom-call | tf_op jit(solution)/shard_map/cond/branch_0_fun/whole/pallas_call | solution.py:327
  97.2 0.8 copy.23
  98.0 0.7 copy.24
  98.7 0.7 copy.25
  (1 shorter events, 0.0 us)
Async XLA Ops:
  0.6 3.6 %copy-start = (bf16[256,4,128]{2,1,0:T(4,128)(2,1)S(1)}, bf16[256,4,128]{2,1,0:T(4,128)(2,1)}, u32[]{:S(2)}) copy-start(bf16[256,4,128]{2,1,0:T(4,128)(2,1)} %param.9) | copy-start | bytes 786436
  4.1 0.7 copy-start.1

commit v2 on v1

--- a/solution.py
+++ b/solution.py
@@ -23,13 +23,26 @@
     return lax.dot_general(a, b, (((1,), (0,)), ((), ())), preferred_element_type=F32)
 
 
-def tile_grads(q, do, qt, dot_t, lse2, delta, k, v, kt, keep=None):
-    e = dot(k, qt) * (SCALE * LOG2E) - lse2
-    if keep is not None:
-        e = jnp.where(keep, e, -jnp.inf)
-    p = jnp.exp2(e)
-    ds = (p * (dot(v, dot_t) - delta)).astype(BF16)
-    return dot(kt, ds), dot(ds, q), dot(p.astype(BF16), do)
+def pipelined(chunks):
+    made = chunks[0][0]()
+    for n, (_, middle, end) in enumerate(chunks):
+        following = chunks[n + 1][0]() if n + 1 < len(chunks) else None
+        end(middle(*made))
+        made = following
+
+
+def chunk(q, do, qt, dot_t, lse2, delta, k, v, end, keep=None):
+    def first():
+        return dot(k(), qt()), dot(v(), dot_t())
+
+    def middle(s, dp):
+        e = s * (SCALE * LOG2E) - lse2()
+        if keep is not None:
+            e = jnp.where(keep, e, -jnp.inf)
+        p = jnp.exp2(e)
+        return p.astype(BF16), (p * (dp - delta())).astype(BF16)
+
+    return first, middle, end
 
 
 def kernel(
@@ -87,13 +100,22 @@
     right_sum = [send(qtx.at[RIGHT, j], qrx.at[0, j], right) for j in (1, 0)]
     left_sum = [send(qtx.at[LEFT, j], qrx.at[1, j], left) for j in (0, 1)]
 
+    def lse_row(columns):
+        shape = (BLK, ROWS)
+        column = lax.broadcasted_iota(jnp.int32, shape, 1)
+        spread = jnp.broadcast_to(columns[:, 0:1], shape)
+        for head in range(1, 4):
+            spread = jnp.where(column % 4 == head, jnp.broadcast_to(columns[:, head : head + 1], shape), spread)
+        mine = column // 4 == lax.broadcasted_iota(jnp.int32, shape, 0)
+        return jnp.sum(jnp.where(mine, spread, 0.0), axis=0, keepdims=True)
+
     kv[0, 0, 0] = k_in[...]
     kv[0, 0, 1] = v_in[...]
     for j in range(2):
         qd0[j, 0] = q_in[j]
         qd0[j, 1] = do_in[j]
         product = do_in[j].astype(F32) * out_in[j].astype(F32)
-        rw0[j, 0] = lse_in[j] * LOG2E
+        rw0[j, 0] = lse_row(lse_in[:, j * BLK : j * BLK + BLK].T) * LOG2E
         rw0[j, 1] = jnp.sum(product.T, axis=0, keepdims=True)
 
     barrier = pltpu.get_barrier_semaphore()
@@ -118,76 +140,152 @@
     dqa[...] = jnp.zeros_like(dqa)
     dka[...] = jnp.zeros_like(dka)
 
-    def query_side(i, j):
-        return qds[i][j, 0], qds[i][j, 1], qts[i][j, 0], qts[i][j, 1]
-
-    for j in range(2):
-        keys = BLK * (j + 1)
-        shape = (keys, ROWS)
-        keep = lax.broadcasted_iota(jnp.int32, shape, 0) <= (
-            lax.broadcasted_iota(jnp.int32, shape, 1) // 4 + j * BLK
+    def halves(i, j, h):
+        cut = slice(h * TOK, h * TOK + TOK)
+        return (
+            lambda: qds[i][j, 0, cut], lambda: qds[i][j, 1, cut],
+            lambda: qts[i][j, 0, :, cut], lambda: qts[i][j, 1, :, cut],
         )
-        dqt, dk, dv = tile_grads(
-            *query_side(OWN, j), rw0[j, 0], rw0[j, 1],
-            kv[0, 0, 0, :keys], kv[0, 0, 1, :keys], kt[0, 0, :, :keys], keep,
-        )
-        dqa[OWN, j] += dqt
-        dka[0, 0, 0, :keys] += dk
-        dka[0, 0, 1, :keys] += dv
+
+    def row(i, j, kind, h):
+        return lambda: rws[i][j, kind, :, h * TOK : h * TOK + TOK]
+
+    def own_chunks():
+        chunks = []
+        for j in range(2):
+            keys = BLK * (j + 1)
+            for h in range(2):
+                shape = (keys, TOK)
+                keep = lax.broadcasted_iota(jnp.int32, shape, 0) <= (
+                    (lax.broadcasted_iota(jnp.int32, shape, 1) + h * TOK) // 4 + j * BLK
+                )
+
+                def end(made, j=j, h=h, keys=keys):
+                    p, ds = made
+                    cut = slice(h * TOK, h * TOK + TOK)
+                    dqa[OWN, j, :, cut] += dot(kt[0, 0, :, :keys], ds)
+                    dka[0, 0, 0, :keys] += dot(ds, qd0[j, 0, cut])
+                    dka[0, 0, 1, :keys] += dot(p, qd0[j, 1, cut])
+
+                chunks.append(
+                    chunk(
+                        *halves(OWN, j, h), row(OWN, j, 0, h), row(OWN, j, 1, h),
+                        lambda keys=keys: kv[0, 0, 0, :keys], lambda keys=keys: kv[0, 0, 1, :keys], end, keep,
+                    )
+                )
+        return chunks
 
     def first_block(i, o, j):
         owner = x * (NY * NZ) + (y + j) % NY * NZ + (z + o) % NZ
         return order[2 * owners[i]], order[2 * owner]
 
     def folded(i, o, parts):
-        lo = [kv[o, j, :, :BLK] for j in parts]
-        dqt, dk, dv = tile_grads(
-            *query_side(i, 1), rws[i][1, 0], rws[i][1, 1],
-            jnp.concatenate([part[0] for part in lo], axis=0),
-            jnp.concatenate([part[1] for part in lo], axis=0),
-            jnp.concatenate([kt[o, j, :, :BLK] for j in parts], axis=1),
-        )
-        early = jnp.zeros((BLK, ROWS), F32)
+        size = BLK * len(parts)
+        state = {"p": [], "ds": [], "dsb": []}
+        chunks = []
+
+        def stack(index):
+            return lambda: jnp.concatenate([kv[o, j, index, :BLK] for j in parts], axis=0)
+
+        def end_later(made, h):
+            state["p"].append(made[0])
+            state["ds"].append(made[1])
+            if h == 1:
+                p = jnp.concatenate(state["p"], axis=1)
+                ds = jnp.concatenate(state["ds"], axis=1)
+                state["dv"] = dot(p, qds[i][1, 1])
+                state["dk"] = dot(ds, qds[i][1, 0])
+                state["dq"] = dot(jnp.concatenate([kt[o, j, :, :BLK] for j in parts], axis=1), ds)
+
+        for h in range(2):
+            chunks.append(
+                chunk(
+                    *halves(i, 1, h), row(i, 1, 0, h), row(i, 1, 1, h), stack(0), stack(1),
+                    functools.partial(end_later, h=h),
+                )
+            )
+
+        weights = []
         for n, j in enumerate(parts):
             query_first, key_first = first_block(i, o, j)
             later = query_first < key_first
             slot = later.astype(jnp.int32)
             weight = later.astype(F32)
-            dqb, dkb, dvb = tile_grads(
-                *query_side(i, slot), rws[i][slot, 0], rws[i][slot, 1],
-                lax.select(later, kv[o, j, 0, BLK:], kv[o, j, 0, :BLK]),
-                lax.select(later, kv[o, j, 1, BLK:], kv[o, j, 1, :BLK]),
-                lax.select(later, kt[o, j, :, BLK:], kt[o, j, :, :BLK]),
+            weights.append(weight)
+
+            def pick(index, later=later, j=j):
+                return lambda: lax.select(later, kv[o, j, index, BLK:], kv[o, j, index, :BLK])
+
+            def end_same(made, n=n, j=j, slot=slot, weight=weight, later=later):
+                p, ds = made
+                dv, dk = dot(p, qds[i][slot, 1]), dot(ds, qds[i][slot, 0])
+                rows = slice(n * BLK, n * BLK + BLK)
+                late_dk, late_dv = weight * dk, weight * dv
+                dka[o, j, 0, :BLK] += state["dk"][rows] + (dk - late_dk)
+                dka[o, j, 1, :BLK] += state["dv"][rows] + (dv - late_dv)
+                dka[o, j, 0, BLK:] += late_dk
+                dka[o, j, 1, BLK:] += late_dv
+                state["dsb"].append(ds)
+                if n == len(parts) - 1:
+                    turned = []
+                    for m, (jm, wm) in enumerate(zip(parts, weights)):
+                        late = kt[o, jm, :, BLK:] * wm.astype(BF16)
+                        early = kt[o, jm, :, :BLK] * (1.0 - wm).astype(BF16)
+                        turned.append(jnp.concatenate([late, early], axis=0))
+                    both = dot(jnp.concatenate(turned, axis=1), jnp.concatenate(state["dsb"], axis=0))
+                    dqa[i, 1] += state["dq"] + both[:BLK]
+                    dqa[i, 0] += both[BLK:]
+
+            chunks.append(
+                chunk(
+                    None, None,
+                    lambda slot=slot: qts[i][slot, 0], lambda slot=slot: qts[i][slot, 1],
+                    lambda slot=slot: rws[i][slot, 0], lambda slot=slot: rws[i][slot, 1],
+                    pick(0), pick(1), end_same,
+                )
             )
-            dqt = dqt + weight * dqb
-            early = early + (1.0 - weight) * dqb
-            rows = slice(n * BLK, n * BLK + BLK)
-            dka[o, j, 0, :BLK] += dk[rows] + (1.0 - weight) * dkb
-            dka[o, j, 1, :BLK] += dv[rows] + (1.0 - weight) * dvb
-            dka[o, j, 0, BLK:] += weight * dkb
-            dka[o, j, 1, BLK:] += weight * dvb
-        dqa[i, 0] += early
-        dqa[i, 1] += dqt
+        return chunks
 
     def whole(i, o, parts):
+        chunks = []
         for j in parts:
             query_first, key_first = first_block(i, o, j)
             hidden = jnp.where(query_first > key_first, 0.0, 1e30).astype(F32)
+            state = {"p": [], "ds": []}
             for slot in range(2):
-                dqt, dk, dv = tile_grads(
-                    *query_side(i, slot), rws[i][slot, 0] + hidden, rws[i][slot, 1],
-                    kv[o, j, 0], kv[o, j, 1], kt[o, j],
-                )
-                dqa[i, slot] += dqt
-                dka[o, j, 0] += dk
-                dka[o, j, 1] += dv
-
-    work = folded if fold else whole
+                for h in range(2):
+                    def end(made, slot=slot, h=h, j=j, state=state):
+                        state["p"].append(made[0])
+                        state["ds"].append(made[1])
+                        if h == 1:
+                            ds = jnp.concatenate(state["ds"][-2:], axis=1)
+                            dqa[i, slot] += dot(kt[o, j], ds)
+                        if h == 1 and slot == 1:
+                            p = jnp.concatenate(state["p"], axis=1)
+                            ds = jnp.concatenate(state["ds"], axis=1)
+                            dka[o, j, 1] += dot(p, jnp.concatenate([qds[i][0, 1], qds[i][1, 1]], axis=0))
+                            dka[o, j, 0] += dot(ds, jnp.concatenate([qds[i][0, 0], qds[i][1, 0]], axis=0))
+
+                    lse2 = row(i, slot, 0, h)
+                    chunks.append(
+                        chunk(
+                            *halves(i, slot, h), lambda lse2=lse2, hidden=hidden: lse2() + hidden, row(i, slot, 1, h),
+                            lambda j=j: kv[o, j, 0], lambda j=j: kv[o, j, 1], end,
+                        )
+                    )
+        return chunks
+
+    step = folded if fold else whole
+
+    def work(*steps):
+        pipelined([c for i, o, parts in steps for c in step(i, o, parts)])
+
+    pipelined(own_chunks())
 
     arrive(across)
     begin(up_kv[0][1], down_kv[0][1])
     kt[0, 1] = kv[0, 1, 0].T
-    work(OWN, 0, (1,))
+    work((OWN, 0, (1,)))
 
     def near(s, carry):
         for hop in (1, 2):
@@ -196,13 +294,10 @@
                 arrive(*up_kv[hop - 1], *down_kv[hop - 1])
                 begin(*up_kv[hop], *down_kv[hop])
 
-        def side(t, carry):
-            o = s + t * (NZ - 2 * s)
-            turn_keys(o)
-            work(OWN, o, (0, 1))
-            return carry
-
-        return lax.fori_loop(0, 2, side, carry)
+        turn_keys(s)
+        turn_keys(NZ - s)
+        work((OWN, s, (0, 1)), (OWN, NZ - s, (0, 1)))
+        return carry
 
     lax.fori_loop(1, 3, near, jnp.int32(0))
 
@@ -220,8 +315,7 @@
 
         s = 1 + t // 2
         o = s + t % 2 * (NZ - 2 * s)
-        work(LEFT, o, (0, 1))
-        work(RIGHT, o, (0, 1))
+        work((LEFT, o, (0, 1)), (RIGHT, o, (0, 1)))
         return carry
 
     lax.fori_loop(0, 4, sides, jnp.int32(0))
@@ -233,17 +327,9 @@
     turn_keys(3)
     turn_keys(5)
 
-    def last(t, carry):
-        s = 4 - (t + 1) // 2
-        o = s + (1 - t % 2) * (NZ - 2 * s)
-
-        @pl.when(t < 3)
-        def _():
-            work(OWN, o, (0, 1))
-            work(LEFT, o, (0, 1))
-            work(RIGHT, o, (0, 1))
-
-        work(OPP, o, (0, 1))
+    def far(t, carry):
+        o = 4 - t + t // 2 * 3
+        work((OWN, o, (0, 1)), (LEFT, o, (0, 1)), (RIGHT, o, (0, 1)), (OPP, o, (0, 1)))
 
         @pl.when(t == 0)
         def _():
@@ -264,27 +350,30 @@
             ktx[5, 1] = (dka[5, 1] + kdn[3, 1].astype(F32)).astype(BF16)
             begin(down_sum[3])
 
+        return carry
+
+    lax.fori_loop(0, 3, far, jnp.int32(0))
+
+    def opposite(t, carry):
+        s = 2 - t
+        work((OPP, s, (0, 1)), (OPP, NZ - s, (0, 1)))
         for hop in (2, 1):
-            @pl.when(t == 7 - 2 * hop)
+            @pl.when(s == hop)
             def _():
                 arrive(up_sum[hop + 1])
                 ktx[hop] = (dka[hop] + kup[hop].astype(F32)).astype(BF16)
                 begin(up_sum[hop])
-
-            @pl.when(t == 8 - 2 * hop)
-            def _():
                 arrive(down_sum[hop + 1])
                 ktx[8 - hop] = (dka[8 - hop] + kdn[hop].astype(F32)).astype(BF16)
                 begin(down_sum[hop])
 
         return carry
 
-    lax.fori_loop(0, 7, last, jnp.int32(0))
-    work(OPP, 0, (0, 1))
+    lax.fori_loop(0, 2, opposite, jnp.int32(0))
+    work((OPP, 0, (0, 1)))
     qtx[OPP] = dqa[OPP].astype(BF16)
     begin(*opp_sum)
-    work(LEFT, 0, (0, 1))
-    work(RIGHT, 0, (0, 1))
+    work((LEFT, 0, (0, 1)), (RIGHT, 0, (0, 1)))
 
     qtx[RIGHT, 1] = dqa[RIGHT, 1].astype(BF16)
     qtx[LEFT, 0] = dqa[LEFT, 0].astype(BF16)
@@ -362,7 +451,7 @@
         query.reshape(2, ROWS, BLK),
         d_output.reshape(2, ROWS, BLK),
         output.reshape(2, ROWS, BLK),
-        lse.reshape(2, 1, ROWS),
+        lse.T,
         key_proj.reshape(TOK, BLK),
         value.reshape(TOK, BLK),
     )

time: 101 us -> 77.5 us (0.77); the launches traced: 99.3 us -> 77.3 us
  Pallas kernels: 92.2 us -> 71.9 us
  local copies, waits for them, and re-layouts: 4.89 us -> 3.34 us
    pallas_call x1, Pallas kernels: 92.2 us -> 71.9 us  [grads(): pl.pallas_call(functools.partial(kernel, fold), out_shape=(jax.ShapeDtype...]
    unnamed x8 -> x7, local copies, waits for them, and re-layouts: 3.45 us -> 2.76 us
where the time goes in v2:
time: 77.5 us; the launch traced here: 77.3 us
  Pallas kernels  71.9 us (93%)
  local copies, waits for them, and re-layouts  3.34 us (4%)
  between operations  1.97 us (3%)
    pallas_call x1, Pallas kernels, grads(): pl.pallas_call(functools.partial(kernel, fold), out_shape=(jax.ShapeDtype...  71.9 us
    unnamed x7, local copies, waits for them, and re-layouts  2.76 us

profile of v2, /device:TPU:16, one launch (start us, length us, event | category | flops | bytes accessed | tf_op | source)
XLA Modules:
  0.0 77.3 jit_solution(16482179045664496576)
XLA Ops:
  0.6 0.0 copy-start.1
  0.6 0.6 copy-done.1
  1.3 0.6 fusion
  1.9 0.0 copy-start
  3.2 0.0 copy-done
  3.2 72.0 %conditional.1 = ((f32[2,512,128]{2,1,0:T(8,128)S(1)}, f32[256,128]{1,0:T(8,128)S(1)}, f32[256,128]{1,0:T(8,128)S(1)})) conditional(s32[]{:T(128)} %bitcast, (s32[128]{0:T(128)S(1)}, bf16[2,512,128]{2,1,0:T(8,128)(2,1)}, bf16[2,512,128]{2,1,0:T(8,128)(2,1)}, bf16[2,512,128]{2,1,0:T(8,128)(2,1)}, f32[4,256]{1,0:T(4,128)S(1)}, ...), branch_computations={%region_0.0_spmd, %region_1.0_spmd} | conditional | bytes 8 | solution.py:459
  3.4 71.9 %folded.1 = (f32[2,512,128]{2,1,0:T(8,128)S(1)}, f32[256,128]{1,0:T(8,128)S(1)}, f32[256,128]{1,0:T(8,128)S(1)}) custom-call(s32[128]{0:T(128)S(1)} %get-tuple-element.47.order, bf16[2,512,128]{2,1,0:T(8,128)(2,1)} %get-tuple-element.48.q_in, bf16[2,512,128]{2,1,0:T(8,128)(2,1)} %get-tuple-element.49.do_in, bf16[2,512,128]{2,1,0:T(8,128)(2,1)} %get-tuple-element.50.out_in, ...), custom_call_target="tpu_custom_call" | custom-call | tf_op jit(solution)/shard_map/cond/branch_1_fun/folded/pallas_call | solution.py:416
  75.2 0.8 %copy.19 = f32[256,4,128]{2,1,0:T(4,128)} copy(f32[256,4,128]{2,1,0:T(4,128)S(1)} %bitcast.16) | data formatting | bytes 1048576
  76.0 0.7 copy.20
  76.7 0.7 copy.21
Async XLA Ops:
  0.6 0.7 copy-start.1
  1.9 1.3 %copy-start = (f32[256,4]{0,1:T(4,128)S(1)}, f32[256,4]{0,1:T(4,128)}, u32[]{:S(2)}) copy-start(f32[256,4]{0,1:T(4,128)} %param.13) | copy-start | bytes 12292

commit v3 on v2

--- a/solution.py
+++ b/solution.py
@@ -16,7 +16,7 @@
 ROWS = 512
 SCALE = BLK ** (-0.5)
 NX, NY, NZ = 4, 2, 8
-OWN, LEFT, RIGHT, OPP = range(4)
+OWN, RIGHT, OPP, LEFT = range(4)
 
 
 def dot(a, b):
@@ -31,7 +31,7 @@
         made = following
 
 
-def chunk(q, do, qt, dot_t, lse2, delta, k, v, end, keep=None):
+def chunk(qt, dot_t, lse2, delta, k, v, end, keep=None):
     def first():
         return dot(k(), qt()), dot(v(), dot_t())
 
@@ -47,7 +47,7 @@
 
 def kernel(
     fold, order, q_in, do_in, out_in, lse_in, k_in, v_in, dq_out, dk_out, dv_out,
-    qd0, qd1, qd2, qd3, qt0, qt1, qt2, qt3, rw0, rw1, rw2, rw3,
+    from_right, from_opp, from_left, rows_right, rows_opp, rows_left, qn, qt, rw,
     kv, kt, dqa, dka, ktx, kup, kdn, ytx, yrx, qtx, qrx, orx, ssem, rsem,
 ):
     ctx = lax.axis_index("ctx")
@@ -55,12 +55,9 @@
     y, z = plane // NZ, plane % NZ
     right = (x + 1) % NX * (NY * NZ) + plane
     left = (x + NX - 1) % NX * (NY * NZ) + plane
-    opp = (x + 2) % NX * (NY * NZ) + plane
     partner = x * (NY * NZ) + (1 - y) * NZ + z
     up = ctx - z + (z + 1) % NZ
     down = ctx - z + (z + NZ - 1) % NZ
-    qds, qts, rws = (qd0, qd1, qd2, qd3), (qt0, qt1, qt2, qt3), (rw0, rw1, rw2, rw3)
-    owners = (ctx, left, right, opp)
     used = []
 
     def send(src, dst, device):
@@ -80,12 +77,12 @@
         for copy in copies:
             copy.wait_recv()
 
-    to_right = [send(qd0.at[j], qd1.at[j], right) for j in range(2)]
-    to_right += [send(rw0, rw1, right)]
-    to_left = [send(qd0.at[j], qd2.at[j], left) for j in range(2)]
-    to_left += [send(rw0, rw2, left)]
-    far_right = [send(qd1.at[0], qd3.at[0], right), send(rw1.at[0], rw3.at[0], right)]
-    far_left = [send(qd2.at[1], qd3.at[1], left), send(rw2.at[1], rw3.at[1], left)]
+    to_right = [send(qn.at[OWN, j], from_left.at[j], right) for j in range(2)]
+    to_right += [send(rw.at[OWN], rows_left, right)]
+    to_left = [send(qn.at[OWN, j], from_right.at[j], left) for j in range(2)]
+    to_left += [send(rw.at[OWN], rows_right, left)]
+    far_right = [send(from_left.at[0], from_opp.at[0], right), send(rows_left.at[0], rows_opp.at[0], right)]
+    far_left = [send(from_right.at[1], from_opp.at[1], left), send(rows_right.at[1], rows_opp.at[1], left)]
     across = send(kv.at[0, 0], kv.at[0, 1], partner)
     up_kv = [[send(kv.at[0, j], kv.at[7, j], up) for j in range(2)]]
     up_kv += [[send(kv.at[8 - s], kv.at[7 - s], up)] for s in (1, 2)] + [[send(kv.at[5, 0], kv.at[4, 0], up)]]
@@ -112,11 +109,11 @@
     kv[0, 0, 0] = k_in[...]
     kv[0, 0, 1] = v_in[...]
     for j in range(2):
-        qd0[j, 0] = q_in[j]
-        qd0[j, 1] = do_in[j]
+        qn[OWN, j, 0] = q_in[j]
+        qn[OWN, j, 1] = do_in[j]
         product = do_in[j].astype(F32) * out_in[j].astype(F32)
-        rw0[j, 0] = lse_row(lse_in[:, j * BLK : j * BLK + BLK].T) * LOG2E
-        rw0[j, 1] = jnp.sum(product.T, axis=0, keepdims=True)
+        rw[OWN, j, 0] = lse_row(lse_in[:, j * BLK : j * BLK + BLK].T) * LOG2E
+        rw[OWN, j, 1] = jnp.sum(product.T, axis=0, keepdims=True)
 
     barrier = pltpu.get_barrier_semaphore()
     for device in (right, left, partner, up, down):
@@ -126,16 +123,19 @@
     begin(across, up_kv[0][0], down_kv[0][0])
     begin(to_right[0], to_left[1], to_right[2], to_left[2], to_right[1], to_left[0])
 
-    def turn_queries(i):
+    def turn_queries(i, landed, landed_rows):
         for j in range(2):
             for part in range(2):
-                qts[i][j, part] = qds[i][j, part].T
+                if landed is not None:
+                    qn[i, j, part] = landed[j, part]
+                    rw[i, j, part] = landed_rows[j, part]
+                qt[i, j, part] = qn[i, j, part].T
 
     def turn_keys(o):
         for j in range(2):
             kt[o, j] = kv[o, j, 0].T
 
-    turn_queries(OWN)
+    turn_queries(OWN, None, None)
     kt[0, 0] = kv[0, 0, 0].T
     dqa[...] = jnp.zeros_like(dqa)
     dka[...] = jnp.zeros_like(dka)
@@ -143,12 +143,11 @@
     def halves(i, j, h):
         cut = slice(h * TOK, h * TOK + TOK)
         return (
-            lambda: qds[i][j, 0, cut], lambda: qds[i][j, 1, cut],
-            lambda: qts[i][j, 0, :, cut], lambda: qts[i][j, 1, :, cut],
+            lambda: qt[i, j, 0, :, cut], lambda: qt[i, j, 1, :, cut],
         )
 
     def row(i, j, kind, h):
-        return lambda: rws[i][j, kind, :, h * TOK : h * TOK + TOK]
+        return lambda: rw[i, j, kind, :, h * TOK : h * TOK + TOK]
 
     def own_chunks():
         chunks = []
@@ -164,8 +163,8 @@
                     p, ds = made
                     cut = slice(h * TOK, h * TOK + TOK)
                     dqa[OWN, j, :, cut] += dot(kt[0, 0, :, :keys], ds)
-                    dka[0, 0, 0, :keys] += dot(ds, qd0[j, 0, cut])
-                    dka[0, 0, 1, :keys] += dot(p, qd0[j, 1, cut])
+                    dka[0, 0, 0, :keys] += dot(ds, qn[OWN, j, 0, cut])
+                    dka[0, 0, 1, :keys] += dot(p, qn[OWN, j, 1, cut])
 
                 chunks.append(
                     chunk(
@@ -177,7 +176,7 @@
 
     def first_block(i, o, j):
         owner = x * (NY * NZ) + (y + j) % NY * NZ + (z + o) % NZ
-        return order[2 * owners[i]], order[2 * owner]
+        return order[2 * ((x + i) % NX * (NY * NZ) + plane)], order[2 * owner]
 
     def folded(i, o, parts):
         size = BLK * len(parts)
@@ -193,8 +192,8 @@
             if h == 1:
                 p = jnp.concatenate(state["p"], axis=1)
                 ds = jnp.concatenate(state["ds"], axis=1)
-                state["dv"] = dot(p, qds[i][1, 1])
-                state["dk"] = dot(ds, qds[i][1, 0])
+                state["dv"] = dot(p, qn[i, 1, 1])
+                state["dk"] = dot(ds, qn[i, 1, 0])
                 state["dq"] = dot(jnp.concatenate([kt[o, j, :, :BLK] for j in parts], axis=1), ds)
 
         for h in range(2):
@@ -218,7 +217,7 @@
 
             def end_same(made, n=n, j=j, slot=slot, weight=weight, later=later):
                 p, ds = made
-                dv, dk = dot(p, qds[i][slot, 1]), dot(ds, qds[i][slot, 0])
+                dv, dk = dot(p, qn[i, slot, 1]), dot(ds, qn[i, slot, 0])
                 rows = slice(n * BLK, n * BLK + BLK)
                 late_dk, late_dv = weight * dk, weight * dv
                 dka[o, j, 0, :BLK] += state["dk"][rows] + (dk - late_dk)
@@ -238,41 +237,44 @@
 
             chunks.append(
                 chunk(
-                    None, None,
-                    lambda slot=slot: qts[i][slot, 0], lambda slot=slot: qts[i][slot, 1],
-                    lambda slot=slot: rws[i][slot, 0], lambda slot=slot: rws[i][slot, 1],
+                    lambda slot=slot: qt[i, slot, 0], lambda slot=slot: qt[i, slot, 1],
+                    lambda slot=slot: rw[i, slot, 0], lambda slot=slot: rw[i, slot, 1],
                     pick(0), pick(1), end_same,
                 )
             )
         return chunks
 
     def whole(i, o, parts):
-        chunks = []
+        hidden = []
         for j in parts:
             query_first, key_first = first_block(i, o, j)
-            hidden = jnp.where(query_first > key_first, 0.0, 1e30).astype(F32)
+            hidden.append(jnp.where(query_first > key_first, 0.0, 1e30).astype(F32))
+        chunks = []
+
+        def stack(index):
+            return lambda: jnp.concatenate([kv[o, j, index] for j in parts], axis=0)
+
+        for slot in range(2):
             state = {"p": [], "ds": []}
-            for slot in range(2):
-                for h in range(2):
-                    def end(made, slot=slot, h=h, j=j, state=state):
-                        state["p"].append(made[0])
-                        state["ds"].append(made[1])
-                        if h == 1:
-                            ds = jnp.concatenate(state["ds"][-2:], axis=1)
-                            dqa[i, slot] += dot(kt[o, j], ds)
-                        if h == 1 and slot == 1:
-                            p = jnp.concatenate(state["p"], axis=1)
-                            ds = jnp.concatenate(state["ds"], axis=1)
-                            dka[o, j, 1] += dot(p, jnp.concatenate([qds[i][0, 1], qds[i][1, 1]], axis=0))
-                            dka[o, j, 0] += dot(ds, jnp.concatenate([qds[i][0, 0], qds[i][1, 0]], axis=0))
-
-                    lse2 = row(i, slot, 0, h)
-                    chunks.append(
-                        chunk(
-                            *halves(i, slot, h), lambda lse2=lse2, hidden=hidden: lse2() + hidden, row(i, slot, 1, h),
-                            lambda j=j: kv[o, j, 0], lambda j=j: kv[o, j, 1], end,
-                        )
-                    )
+            for h in range(2):
+                lse2 = row(i, slot, 0, h)
+
+                def penalised(lse2=lse2):
+                    return jnp.concatenate([jnp.broadcast_to(lse2() + up, (TOK, TOK)) for up in hidden], axis=0)
+
+                def end(made, slot=slot, h=h, state=state):
+                    state["p"].append(made[0])
+                    state["ds"].append(made[1])
+                    cut = slice(h * TOK, h * TOK + TOK)
+                    dqa[i, slot, :, cut] += dot(jnp.concatenate([kt[o, j] for j in parts], axis=1), made[1])
+                    if h == 1:
+                        dv = dot(jnp.concatenate(state["p"], axis=1), qn[i, slot, 1])
+                        dk = dot(jnp.concatenate(state["ds"], axis=1), qn[i, slot, 0])
+                        for n, j in enumerate(parts):
+                            dka[o, j, 0] += dk[n * TOK : n * TOK + TOK]
+                            dka[o, j, 1] += dv[n * TOK : n * TOK + TOK]
+
+                chunks.append(chunk(*halves(i, slot, h), penalised, row(i, slot, 1, h), stack(0), stack(1), end))
         return chunks
 
     step = folded if fold else whole
@@ -287,78 +289,72 @@
     kt[0, 1] = kv[0, 1, 0].T
     work((OWN, 0, (1,)))
 
-    def near(s, carry):
-        for hop in (1, 2):
-            @pl.when(s == hop)
-            def _():
-                arrive(*up_kv[hop - 1], *down_kv[hop - 1])
-                begin(*up_kv[hop], *down_kv[hop])
-
-        turn_keys(s)
-        turn_keys(NZ - s)
-        work((OWN, s, (0, 1)), (OWN, NZ - s, (0, 1)))
-        return carry
-
-    lax.fori_loop(1, 3, near, jnp.int32(0))
-
-    arrive(to_right[0], to_right[2], to_left[1], to_left[2])
-    begin(*far_right, *far_left)
-    arrive(to_right[1], to_left[0])
-    turn_queries(LEFT)
-    turn_queries(RIGHT)
-
-    def sides(t, carry):
+    table = [
+        (OWN, 1, OWN, 7), (OWN, 2, OWN, 6),
+        (LEFT, 1, RIGHT, 1), (LEFT, 7, RIGHT, 7), (LEFT, 2, RIGHT, 2), (LEFT, 6, RIGHT, 6),
+        (OWN, 4, LEFT, 4), (RIGHT, 4, OPP, 4), (OWN, 3, LEFT, 3), (RIGHT, 3, OPP, 3), (OWN, 5, LEFT, 5), (RIGHT, 5, OPP, 5),
+        (OPP, 2, OPP, 6), (OPP, 1, OPP, 7), (OPP, 0, LEFT, 0),
+    ]
+
+    def before(t):
+        @pl.when(t == 0)
+        def _():
+            arrive(*up_kv[0], *down_kv[0])
+            begin(*up_kv[1], *down_kv[1])
+            turn_keys(1)
+            turn_keys(7)
+
+        @pl.when(t == 1)
+        def _():
+            arrive(*up_kv[1], *down_kv[1])
+            begin(*up_kv[2], *down_kv[2])
+            turn_keys(2)
+            turn_keys(6)
+
         @pl.when(t == 2)
+        def _():
+            arrive(to_right[0], to_right[2], to_left[1], to_left[2])
+            begin(*far_right, *far_left)
+            arrive(to_right[1], to_left[0])
+            turn_queries(LEFT, from_left, rows_left)
+            turn_queries(RIGHT, from_right, rows_right)
+
+        @pl.when(t == 4)
         def _():
             arrive(*up_kv[2], *down_kv[2])
             begin(*up_kv[3], *down_kv[3])
-
-        s = 1 + t // 2
-        o = s + t % 2 * (NZ - 2 * s)
-        work((LEFT, o, (0, 1)), (RIGHT, o, (0, 1)))
-        return carry
-
-    lax.fori_loop(0, 4, sides, jnp.int32(0))
-
-    arrive(*far_right, *far_left)
-    turn_queries(OPP)
-    arrive(*up_kv[3], *down_kv[3])
-    turn_keys(4)
-    turn_keys(3)
-    turn_keys(5)
-
-    def far(t, carry):
-        o = 4 - t + t // 2 * 3
-        work((OWN, o, (0, 1)), (LEFT, o, (0, 1)), (RIGHT, o, (0, 1)), (OPP, o, (0, 1)))
-
-        @pl.when(t == 0)
+            turn_keys(3)
+            turn_keys(5)
+
+        @pl.when(t == 6)
+        def _():
+            arrive(*far_right, *far_left)
+            turn_queries(OPP, from_opp, rows_opp)
+            arrive(*up_kv[3], *down_kv[3])
+            turn_keys(4)
+
+    def after(t):
+        @pl.when(t == 7)
         def _():
             ktx[4] = dka[4].astype(BF16)
             begin(up_sum[4], down_sum[4])
 
-        @pl.when(t == 1)
+        @pl.when(t == 9)
         def _():
             ktx[3, 1] = dka[3, 1].astype(BF16)
             arrive(up_sum[4])
             ktx[3, 0] = (dka[3, 0] + kup[3, 0].astype(F32)).astype(BF16)
             begin(up_sum[3])
 
-        @pl.when(t == 2)
+        @pl.when(t == 11)
         def _():
             ktx[5, 0] = dka[5, 0].astype(BF16)
             arrive(down_sum[4])
             ktx[5, 1] = (dka[5, 1] + kdn[3, 1].astype(F32)).astype(BF16)
             begin(down_sum[3])
 
-        return carry
-
-    lax.fori_loop(0, 3, far, jnp.int32(0))
-
-    def opposite(t, carry):
-        s = 2 - t
-        work((OPP, s, (0, 1)), (OPP, NZ - s, (0, 1)))
         for hop in (2, 1):
-            @pl.when(s == hop)
+            @pl.when(t == 14 - hop)
             def _():
                 arrive(up_sum[hop + 1])
                 ktx[hop] = (dka[hop] + kup[hop].astype(F32)).astype(BF16)
@@ -367,13 +363,25 @@
                 ktx[8 - hop] = (dka[8 - hop] + kdn[hop].astype(F32)).astype(BF16)
                 begin(down_sum[hop])
 
+        @pl.when(t == 14)
+        def _():
+            qtx[OPP] = dqa[OPP].astype(BF16)
+            begin(*opp_sum)
+
+    def both(t, carry):
+        packed = jnp.int32(0)
+        for n, (ia, oa, ib, ob) in enumerate(table):
+            packed = jnp.where(t == n, jnp.int32(ia + 4 * oa + 32 * ib + 128 * ob), packed)
+        pl.when(t < 7)(lambda: before(t))
+        work(
+            (packed % 4, packed // 4 % 8, (0, 1)),
+            (packed // 32 % 4, packed // 128, (0, 1)),
+        )
+        pl.when(t > 6)(lambda: after(t))
         return carry
 
-    lax.fori_loop(0, 2, opposite, jnp.int32(0))
-    work((OPP, 0, (0, 1)))
-    qtx[OPP] = dqa[OPP].astype(BF16)
-    begin(*opp_sum)
-    work((LEFT, 0, (0, 1)), (RIGHT, 0, (0, 1)))
+    lax.fori_loop(0, len(table), both, jnp.int32(0))
+    work((RIGHT, 0, (0, 1)))
 
     qtx[RIGHT, 1] = dqa[RIGHT, 1].astype(BF16)
     qtx[LEFT, 0] = dqa[LEFT, 0].astype(BF16)
@@ -410,9 +418,12 @@
 def grads(fold, order, q, do, out, lse, k, v):
     smem = pl.BlockSpec(memory_space=pltpu.SMEM)
     vmem = pl.BlockSpec(memory_space=pltpu.VMEM)
-    queries = [pltpu.VMEM((2, 2, ROWS, BLK), BF16)] * 4
-    turned = [pltpu.VMEM((2, 2, BLK, ROWS), BF16)] * 4
-    rows = [pltpu.VMEM((2, 2, 1, ROWS), F32)] * 4
+    landing = [pltpu.VMEM((2, 2, ROWS, BLK), BF16)] * 3 + [pltpu.VMEM((2, 2, 1, ROWS), F32)] * 3
+    queries = [
+        pltpu.VMEM((4, 2, 2, ROWS, BLK), BF16),
+        pltpu.VMEM((4, 2, 2, BLK, ROWS), BF16),
+        pltpu.VMEM((4, 2, 2, 1, ROWS), F32),
+    ]
     return pl.pallas_call(
         functools.partial(kernel, fold),
         out_shape=(
@@ -422,7 +433,7 @@
         ),
         in_specs=[smem] + [vmem] * 6,
         out_specs=(vmem, vmem, vmem),
-        scratch_shapes=queries + turned + rows + [
+        scratch_shapes=landing + queries + [
             pltpu.VMEM((NZ, NY, 2, TOK, BLK), BF16),
             pltpu.VMEM((NZ, NY, BLK, TOK), BF16),
             pltpu.VMEM((4, 2, BLK, ROWS), F32),

time: 77.5 us -> 79 us (1.019); the launches traced: 77.3 us -> 77.9 us
  no operation moved by 1% of the time
where the time goes in v3:
time: 79 us; the launch traced here: 77.9 us
  Pallas kernels  72.4 us (92%)
  local copies, waits for them, and re-layouts  3.34 us (4%)
  between operations  1.97 us (2%)
    pallas_call x1, Pallas kernels, grads(): pl.pallas_call(functools.partial(kernel, fold), out_shape=(jax.ShapeDtype...  72.4 us
    unnamed x7, local copies, waits for them, and re-layouts  2.76 us

profile of v3, /device:TPU:16, one launch (start us, length us, event | category | flops | bytes accessed | tf_op | source)
XLA Modules:
  0.0 77.9 jit_solution(4069962629987407492)
XLA Ops:
  0.6 0.0 copy-start.1
  0.6 0.6 copy-done.1
  1.3 0.6 fusion
  1.9 0.0 copy-start
  3.2 0.0 copy-done
  3.2 72.6 %conditional.1 = ((f32[2,512,128]{2,1,0:T(8,128)S(1)}, f32[256,128]{1,0:T(8,128)S(1)}, f32[256,128]{1,0:T(8,128)S(1)})) conditional(s32[]{:T(128)} %bitcast, (s32[128]{0:T(128)S(1)}, bf16[2,512,128]{2,1,0:T(8,128)(2,1)}, bf16[2,512,128]{2,1,0:T(8,128)(2,1)}, bf16[2,512,128]{2,1,0:T(8,128)(2,1)}, f32[4,256]{1,0:T(4,128)S(1)}, ...), branch_computations={%region_0.0_spmd, %region_1.0_spmd} | conditional | bytes 8 | solution.py:470
  3.4 72.4 %folded.1 = (f32[2,512,128]{2,1,0:T(8,128)S(1)}, f32[256,128]{1,0:T(8,128)S(1)}, f32[256,128]{1,0:T(8,128)S(1)}) custom-call(s32[128]{0:T(128)S(1)} %get-tuple-element.47.order, bf16[2,512,128]{2,1,0:T(8,128)(2,1)} %get-tuple-element.48.q_in, bf16[2,512,128]{2,1,0:T(8,128)(2,1)} %get-tuple-element.49.do_in, bf16[2,512,128]{2,1,0:T(8,128)(2,1)} %get-tuple-element.50.out_in, ...), custom_call_target="tpu_custom_call" | custom-call | tf_op jit(solution)/shard_map/cond/branch_1_fun/folded/pallas_call | solution.py:427
  75.8 0.8 %copy.19 = f32[256,4,128]{2,1,0:T(4,128)} copy(f32[256,4,128]{2,1,0:T(4,128)S(1)} %bitcast.16) | data formatting | bytes 1048576
  76.6 0.7 copy.20
  77.2 0.7 copy.21
Async XLA Ops:
  0.6 0.7 copy-start.1
  1.9 1.3 %copy-start = (f32[256,4]{0,1:T(4,128)S(1)}, f32[256,4]{0,1:T(4,128)}, u32[]{:S(2)}) copy-start(f32[256,4]{0,1:T(4,128)} %param.13) | copy-start | bytes 12292

commit v4 on v3

--- a/solution.py
+++ b/solution.py
@@ -24,10 +24,12 @@
 
 
 def pipelined(chunks):
-    made = chunks[0][0]()
-    for n, (_, middle, end) in enumerate(chunks):
-        following = chunks[n + 1][0]() if n + 1 < len(chunks) else None
-        end(middle(*made))
+    made = chunks[0][1](*chunks[0][0]())
+    for n, (_, _, end) in enumerate(chunks):
+        following = None
+        if n + 1 < len(chunks):
+            following = chunks[n + 1][1](*chunks[n + 1][0]())
+        end(made)
         made = following
 
 
@@ -48,7 +50,7 @@
 def kernel(
     fold, order, q_in, do_in, out_in, lse_in, k_in, v_in, dq_out, dk_out, dv_out,
     from_right, from_opp, from_left, rows_right, rows_opp, rows_left, qn, qt, rw,
-    kv, kt, dqa, dka, ktx, kup, kdn, ytx, yrx, qtx, qrx, orx, ssem, rsem,
+    kv, kt, dqa, dka, ktx, kup, kdn, ytx, yrx, qtx, qrx, orx, out_own, lse_own, ssem, rsem, osem,
 ):
     ctx = lax.axis_index("ctx")
     x, plane = ctx // (NY * NZ), ctx % (NY * NZ)
@@ -84,14 +86,14 @@
     far_right = [send(from_left.at[0], from_opp.at[0], right), send(rows_left.at[0], rows_opp.at[0], right)]
     far_left = [send(from_right.at[1], from_opp.at[1], left), send(rows_right.at[1], rows_opp.at[1], left)]
     across = send(kv.at[0, 0], kv.at[0, 1], partner)
-    up_kv = [[send(kv.at[0, j], kv.at[7, j], up) for j in range(2)]]
-    up_kv += [[send(kv.at[8 - s], kv.at[7 - s], up)] for s in (1, 2)] + [[send(kv.at[5, 0], kv.at[4, 0], up)]]
-    down_kv = [[send(kv.at[0, j], kv.at[1, j], down) for j in range(2)]]
-    down_kv += [[send(kv.at[s], kv.at[s + 1], down)] for s in (1, 2)] + [[send(kv.at[3, 1], kv.at[4, 1], down)]]
-    up_sum = {4: send(ktx.at[4, 0], kup.at[3, 0], up)}
-    up_sum.update({o: send(ktx.at[o], kup.at[o - 1], up) for o in (3, 2, 1)})
-    down_sum = {4: send(ktx.at[4, 1], kdn.at[3, 1], down)}
-    down_sum.update({o: send(ktx.at[8 - o], kdn.at[o - 1], down) for o in (3, 2, 1)})
+    up_kv = [[send(kv.at[-s % NZ, j], kv.at[7 - s, j], up) for j in range(2)] for s in range(3)]
+    up_kv += [[send(kv.at[5, 0], kv.at[4, 0], up)]]
+    down_kv = [[send(kv.at[s, j], kv.at[s + 1, j], down) for j in range(2)] for s in range(3)]
+    down_kv += [[send(kv.at[3, 1], kv.at[4, 1], down)]]
+    up_sum = {4: [send(ktx.at[4, 0], kup.at[3, 0], up)]}
+    up_sum.update({o: [send(ktx.at[o, j], kup.at[o - 1, j], up) for j in range(2)] for o in (3, 2, 1)})
+    down_sum = {4: [send(ktx.at[4, 1], kdn.at[3, 1], down)]}
+    down_sum.update({o: [send(ktx.at[8 - o, j], kdn.at[o - 1, j], down) for j in range(2)] for o in (3, 2, 1)})
     across_sum = send(ytx, yrx, partner)
     opp_sum = [send(qtx.at[OPP, 0], orx.at[0], right), send(qtx.at[OPP, 1], orx.at[1], left)]
     right_sum = [send(qtx.at[RIGHT, j], qrx.at[0, j], right) for j in (1, 0)]
@@ -106,22 +108,35 @@
         mine = column // 4 == lax.broadcasted_iota(jnp.int32, shape, 0)
         return jnp.sum(jnp.where(mine, spread, 0.0), axis=0, keepdims=True)
 
-    kv[0, 0, 0] = k_in[...]
-    kv[0, 0, 1] = v_in[...]
-    for j in range(2):
-        qn[OWN, j, 0] = q_in[j]
-        qn[OWN, j, 1] = do_in[j]
-        product = do_in[j].astype(F32) * out_in[j].astype(F32)
-        rw[OWN, j, 0] = lse_row(lse_in[:, j * BLK : j * BLK + BLK].T) * LOG2E
-        rw[OWN, j, 1] = jnp.sum(product.T, axis=0, keepdims=True)
-
     barrier = pltpu.get_barrier_semaphore()
     for device in (right, left, partner, up, down):
         pl.semaphore_signal(barrier, inc=1, device_id={"ctx": device}, device_id_type=MESH)
+    own = [
+        (k_in, kv.at[0, 0, 0]), (v_in, kv.at[0, 0, 1]),
+        (q_in.at[1], qn.at[OWN, 1, 0]), (do_in.at[1], qn.at[OWN, 1, 1]),
+        (q_in.at[0], qn.at[OWN, 0, 0]), (do_in.at[0], qn.at[OWN, 0, 1]),
+        (out_in, out_own), (lse_in, lse_own),
+    ]
+    own = [pltpu.make_async_copy(src, dst, osem.at[n]) for n, (src, dst) in enumerate(own)]
+    begin(*own)
+    own[0].wait()
+    own[1].wait()
     pl.semaphore_wait(barrier, 5)
-
     begin(across, up_kv[0][0], down_kv[0][0])
-    begin(to_right[0], to_left[1], to_right[2], to_left[2], to_right[1], to_left[0])
+    own[2].wait()
+    own[3].wait()
+    begin(to_left[1], to_right[1])
+    own[4].wait()
+    own[5].wait()
+    begin(to_right[0], to_left[0])
+
+    own[6].wait()
+    own[7].wait()
+    for j in range(2):
+        product = qn[OWN, j, 1].astype(F32) * out_own[j].astype(F32)
+        rw[OWN, j, 0] = lse_row(lse_own[:, j * BLK : j * BLK + BLK].T) * LOG2E
+        rw[OWN, j, 1] = jnp.sum(product.T, axis=0, keepdims=True)
+    begin(to_right[2], to_left[2])
 
     def turn_queries(i, landed, landed_rows):
         for j in range(2):
@@ -286,6 +301,8 @@
 
     arrive(across)
     begin(up_kv[0][1], down_kv[0][1])
+    arrive(up_kv[0][0], down_kv[0][0])
+    begin(up_kv[1][0], down_kv[1][0])
     kt[0, 1] = kv[0, 1, 0].T
     work((OWN, 0, (1,)))
 
@@ -299,15 +316,16 @@
     def before(t):
         @pl.when(t == 0)
         def _():
-            arrive(*up_kv[0], *down_kv[0])
-            begin(*up_kv[1], *down_kv[1])
+            arrive(up_kv[0][1], down_kv[0][1])
+            begin(up_kv[1][1], down_kv[1][1])
             turn_keys(1)
             turn_keys(7)
 
         @pl.when(t == 1)
         def _():
-            arrive(*up_kv[1], *down_kv[1])
-            begin(*up_kv[2], *down_kv[2])
+            for j in range(2):
+                arrive(up_kv[1][j], down_kv[1][j])
+                begin(up_kv[2][j], down_kv[2][j])
             turn_keys(2)
             turn_keys(6)
 
@@ -321,8 +339,11 @@
 
         @pl.when(t == 4)
         def _():
-            arrive(*up_kv[2], *down_kv[2])
-            begin(*up_kv[3], *down_kv[3])
+            arrive(up_kv[2][0])
+            begin(*up_kv[3])
+            arrive(down_kv[2][0], down_kv[2][1])
+            begin(*down_kv[3])
+            arrive(up_kv[2][1])
             turn_keys(3)
             turn_keys(5)
 
@@ -337,31 +358,34 @@
         @pl.when(t == 7)
         def _():
             ktx[4] = dka[4].astype(BF16)
-            begin(up_sum[4], down_sum[4])
+            begin(*up_sum[4], *down_sum[4])
 
         @pl.when(t == 9)
         def _():
             ktx[3, 1] = dka[3, 1].astype(BF16)
-            arrive(up_sum[4])
+            begin(up_sum[3][1])
+            arrive(*up_sum[4])
             ktx[3, 0] = (dka[3, 0] + kup[3, 0].astype(F32)).astype(BF16)
-            begin(up_sum[3])
+            begin(up_sum[3][0])
 
         @pl.when(t == 11)
         def _():
             ktx[5, 0] = dka[5, 0].astype(BF16)
-            arrive(down_sum[4])
+            begin(down_sum[3][0])
+            arrive(*down_sum[4])
             ktx[5, 1] = (dka[5, 1] + kdn[3, 1].astype(F32)).astype(BF16)
-            begin(down_sum[3])
+            begin(down_sum[3][1])
 
         for hop in (2, 1):
             @pl.when(t == 14 - hop)
             def _():
-                arrive(up_sum[hop + 1])
-                ktx[hop] = (dka[hop] + kup[hop].astype(F32)).astype(BF16)
-                begin(up_sum[hop])
-                arrive(down_sum[hop + 1])
-                ktx[8 - hop] = (dka[8 - hop] + kdn[hop].astype(F32)).astype(BF16)
-                begin(down_sum[hop])
+                for j in range(2):
+                    arrive(up_sum[hop + 1][1 - j])
+                    ktx[hop, 1 - j] = (dka[hop, 1 - j] + kup[hop, 1 - j].astype(F32)).astype(BF16)
+                    begin(up_sum[hop][1 - j])
+                    arrive(down_sum[hop + 1][j])
+                    ktx[8 - hop, j] = (dka[8 - hop, j] + kdn[hop, j].astype(F32)).astype(BF16)
+                    begin(down_sum[hop][j])
 
         @pl.when(t == 14)
         def _():
@@ -390,9 +414,10 @@
     qtx[RIGHT, 0] = (dqa[RIGHT, 0] + orx[0].astype(F32)).astype(BF16)
     qtx[LEFT, 1] = (dqa[LEFT, 1] + orx[1].astype(F32)).astype(BF16)
     begin(right_sum[1], left_sum[1])
-    arrive(up_sum[1], down_sum[1])
+    arrive(up_sum[1][1], down_sum[1][1])
     ytx[...] = (dka[0, 1] + kup[0, 1].astype(F32) + kdn[0, 1].astype(F32)).astype(BF16)
     begin(across_sum)
+    arrive(up_sum[1][0], down_sum[1][0])
     total = dka[0, 0] + kup[0, 0].astype(F32) + kdn[0, 0].astype(F32)
     arrive(across_sum)
     total = total + yrx[...].astype(F32)
@@ -405,14 +430,14 @@
 
     for copy in to_right + to_left + far_right + far_left + [across, across_sum]:
         copy.wait_send()
-    for group in up_kv + down_kv:
+    for group in up_kv + down_kv + list(up_sum.values()) + list(down_sum.values()):
         for copy in group:
             copy.wait_send()
-    for copy in list(up_sum.values()) + list(down_sum.values()) + opp_sum + right_sum + left_sum:
+    for copy in opp_sum + right_sum + left_sum:
         copy.wait_send()
 
 
-N_COPIES = 3 + 3 + 2 + 2 + 1 + 5 + 5 + 4 + 4 + 1 + 2 + 2 + 2
+N_COPIES = 3 + 3 + 2 + 2 + 1 + 7 + 7 + 7 + 7 + 1 + 2 + 2 + 2
 
 
 def grads(fold, order, q, do, out, lse, k, v):
@@ -431,7 +456,7 @@
             jax.ShapeDtypeStruct((TOK, BLK), F32),
             jax.ShapeDtypeStruct((TOK, BLK), F32),
         ),
-        in_specs=[smem] + [vmem] * 6,
+        in_specs=[smem] + [pl.BlockSpec(memory_space=pltpu.HBM)] * 6,
         out_specs=(vmem, vmem, vmem),
         scratch_shapes=landing + queries + [
             pltpu.VMEM((NZ, NY, 2, TOK, BLK), BF16),
@@ -446,8 +471,11 @@
             pltpu.VMEM((4, 2, BLK, ROWS), BF16),
             pltpu.VMEM((2, 2, BLK, ROWS), BF16),
             pltpu.VMEM((2, BLK, ROWS), BF16),
+            pltpu.VMEM((2, ROWS, BLK), BF16),
+            pltpu.VMEM((4, TOK), F32),
             pltpu.SemaphoreType.DMA((N_COPIES,)),
             pltpu.SemaphoreType.DMA((N_COPIES,)),
+            pltpu.SemaphoreType.DMA((8,)),
         ],
         compiler_params=pltpu.CompilerParams(
             collective_id=0 if fold else 1, has_side_effects=True, vmem_limit_bytes=48 * 1024 * 1024

time: 79 us -> 86.1 us (1.090)
  Pallas kernels: 72.4 us -> 80.1 us
    pallas_call x1, Pallas kernels: 72.4 us -> 80.1 us  [grads(): pl.pallas_call(functools.partial(kernel, fold), out_shape=(jax.ShapeDtype...]
where the time goes in v4:
time: 86.1 us; the launch traced here: 85.6 us
  Pallas kernels  80.1 us (93%)
  local copies, waits for them, and re-layouts  3.34 us (4%)
  between operations  1.97 us (2%)
    pallas_call x1, Pallas kernels, grads(): pl.pallas_call(functools.partial(kernel, fold), out_shape=(jax.ShapeDtype...  80.1 us
    unnamed x7, local copies, waits for them, and re-layouts  2.76 us

profile of v4, /device:TPU:16, one launch (start us, length us, event | category | flops | bytes accessed | tf_op | source)
XLA Modules:
  0.0 85.6 jit_solution(18197799684931329931)
XLA Ops:
  0.6 0.0 copy-start.1
  0.6 0.6 copy-done.1
  1.3 0.6 fusion
  1.9 0.0 copy-start
  3.2 0.0 copy-done
  3.2 80.3 %conditional.1 = ((f32[2,512,128]{2,1,0:T(8,128)S(1)}, f32[256,128]{1,0:T(8,128)S(1)}, f32[256,128]{1,0:T(8,128)S(1)})) conditional(s32[]{:T(128)} %bitcast, (s32[128]{0:T(128)S(1)}, bf16[2,512,128]{2,1,0:T(8,128)(2,1)}, bf16[2,512,128]{2,1,0:T(8,128)(2,1)}, bf16[2,512,128]{2,1,0:T(8,128)(2,1)}, f32[4,256]{1,0:T(4,128)S(1)}, ...), branch_computations={%region_0.0_spmd, %region_1.0_spmd} | conditional | bytes 8 | solution.py:498
  3.2 80.1 %whole.1 = (f32[2,512,128]{2,1,0:T(8,128)S(1)}, f32[256,128]{1,0:T(8,128)S(1)}, f32[256,128]{1,0:T(8,128)S(1)}) custom-call(s32[128]{0:T(128)S(1)} %get-tuple-element.37.order, bf16[2,512,128]{2,1,0:T(8,128)(2,1)} %get-tuple-element.38.q_in, bf16[2,512,128]{2,1,0:T(8,128)(2,1)} %get-tuple-element.39.do_in, bf16[2,512,128]{2,1,0:T(8,128)(2,1)} %get-tuple-element.40.out_in, ...), custom_call_target="tpu_custom_call" | custom-call | tf_op jit(solution)/shard_map/cond/branch_0_fun/whole/pallas_call | solution.py:452
  83.5 0.8 copy.19
  84.3 0.7 copy.20
  85.0 0.7 copy.21
Async XLA Ops:
  0.6 0.7 copy-start.1
  1.9 1.3 %copy-start = (f32[256,4]{0,1:T(4,128)S(1)}, f32[256,4]{0,1:T(4,128)}, u32[]{:S(2)}) copy-start(f32[256,4]{0,1:T(4,128)} %param.13) | copy-start | bytes 12292

commit v5 on v4

--- a/solution.py
+++ b/solution.py
@@ -50,7 +50,7 @@
 def kernel(
     fold, order, q_in, do_in, out_in, lse_in, k_in, v_in, dq_out, dk_out, dv_out,
     from_right, from_opp, from_left, rows_right, rows_opp, rows_left, qn, qt, rw,
-    kv, kt, dqa, dka, ktx, kup, kdn, ytx, yrx, qtx, qrx, orx, out_own, lse_own, ssem, rsem, osem,
+    kv, kt, dqa, dka, ktx, kup, kdn, vrx, yrx, qtx, qrx, orx, out_own, lse_own, ssem, rsem, osem,
 ):
     ctx = lax.axis_index("ctx")
     x, plane = ctx // (NY * NZ), ctx % (NY * NZ)
@@ -86,15 +86,22 @@
     far_right = [send(from_left.at[0], from_opp.at[0], right), send(rows_left.at[0], rows_opp.at[0], right)]
     far_left = [send(from_right.at[1], from_opp.at[1], left), send(rows_right.at[1], rows_opp.at[1], left)]
     across = send(kv.at[0, 0], kv.at[0, 1], partner)
-    up_kv = [[send(kv.at[-s % NZ, j], kv.at[7 - s, j], up) for j in range(2)] for s in range(3)]
+    values = {o: send(kv.at[o, 0, 1], kv.at[o, 1, 1], partner) for o in range(1, NZ)}
+    up_kv = [
+        [send(kv.at[-s % NZ, 0], kv.at[7 - s, 0], up), send(kv.at[-s % NZ, 1, 0], kv.at[7 - s, 1, 0], up)]
+        for s in range(3)
+    ]
     up_kv += [[send(kv.at[5, 0], kv.at[4, 0], up)]]
-    down_kv = [[send(kv.at[s, j], kv.at[s + 1, j], down) for j in range(2)] for s in range(3)]
-    down_kv += [[send(kv.at[3, 1], kv.at[4, 1], down)]]
-    up_sum = {4: [send(ktx.at[4, 0], kup.at[3, 0], up)]}
-    up_sum.update({o: [send(ktx.at[o, j], kup.at[o - 1, j], up) for j in range(2)] for o in (3, 2, 1)})
-    down_sum = {4: [send(ktx.at[4, 1], kdn.at[3, 1], down)]}
-    down_sum.update({o: [send(ktx.at[8 - o, j], kdn.at[o - 1, j], down) for j in range(2)] for o in (3, 2, 1)})
-    across_sum = send(ytx, yrx, partner)
+    down_kv = [
+        [send(kv.at[s, 0], kv.at[s + 1, 0], down), send(kv.at[s, 1, 0], kv.at[s + 1, 1, 0], down)] for s in range(3)
+    ]
+    down_kv += [[send(kv.at[3, 1, 0], kv.at[4, 1, 0], down)]]
+    up_mine = {o: send(ktx.at[o, 0], kup.at[o - 1, 0], up) for o in (4, 3, 2, 1)}
+    up_other = {o: send(ktx.at[o, 1, 0], kup.at[o - 1, 1, 0], up) for o in (3, 2, 1)}
+    down_mine = {o: send(ktx.at[NZ - o, 0], kdn.at[o - 1, 0], down) for o in (3, 2, 1)}
+    down_other = {o: send(ktx.at[NZ - o, 1, 0], kdn.at[o - 1, 1, 0], down) for o in (4, 3, 2, 1)}
+    value_sum = {o: send(ktx.at[o, 1, 1], vrx.at[o], partner) for o in range(NZ)}
+    across_sum = send(ktx.at[0, 1, 0], yrx, partner)
     opp_sum = [send(qtx.at[OPP, 0], orx.at[0], right), send(qtx.at[OPP, 1], orx.at[1], left)]
     right_sum = [send(qtx.at[RIGHT, j], qrx.at[0, j], right) for j in (1, 0)]
     left_sum = [send(qtx.at[LEFT, j], qrx.at[1, j], left) for j in (0, 1)]
@@ -302,7 +309,7 @@
     arrive(across)
     begin(up_kv[0][1], down_kv[0][1])
     arrive(up_kv[0][0], down_kv[0][0])
-    begin(up_kv[1][0], down_kv[1][0])
+    begin(up_kv[1][0], down_kv[1][0], values[7], values[1])
     kt[0, 1] = kv[0, 1, 0].T
     work((OWN, 0, (1,)))
 
@@ -320,14 +327,17 @@
             begin(up_kv[1][1], down_kv[1][1])
             turn_keys(1)
             turn_keys(7)
+            arrive(values[7], values[1])
 
         @pl.when(t == 1)
         def _():
-            for j in range(2):
-                arrive(up_kv[1][j], down_kv[1][j])
-                begin(up_kv[2][j], down_kv[2][j])
+            arrive(up_kv[1][0], down_kv[1][0])
+            begin(up_kv[2][0], down_kv[2][0], values[6], values[2])
+            arrive(up_kv[1][1], down_kv[1][1])
+            begin(up_kv[2][1], down_kv[2][1])
             turn_keys(2)
             turn_keys(6)
+            arrive(values[6], values[2])
 
         @pl.when(t == 2)
         def _():
@@ -337,60 +347,101 @@
             turn_queries(LEFT, from_left, rows_left)
             turn_queries(RIGHT, from_right, rows_right)
 
+        @pl.when(t == 3)
+        def _():
+            arrive(up_kv[2][0])
+            begin(up_kv[3][0], values[5])
+            arrive(down_kv[2][0], down_kv[2][1])
+            begin(down_kv[3][0], values[3])
+
         @pl.when(t == 4)
         def _():
-            arrive(up_kv[2][0])
-            begin(*up_kv[3])
-            arrive(down_kv[2][0], down_kv[2][1])
-            begin(*down_kv[3])
             arrive(up_kv[2][1])
             turn_keys(3)
             turn_keys(5)
 
+        @pl.when(t == 5)
+        def _():
+            arrive(up_kv[3][0])
+            begin(values[4])
+
         @pl.when(t == 6)
         def _():
             arrive(*far_right, *far_left)
             turn_queries(OPP, from_opp, rows_opp)
-            arrive(*up_kv[3], *down_kv[3])
+            arrive(down_kv[3][0])
             turn_keys(4)
+            arrive(values[3], values[5], values[4])
+
+    def start_values(o):
+        ktx[o, 1, 1] = dka[o, 1, 1].astype(BF16)
+        begin(value_sum[o])
+
+    def pass_other(o, out, inbound=None, landed=None):
+        total = dka[o, 1, 0]
+        if inbound is not None:
+            arrive(inbound)
+            total = total + landed[1, 0].astype(F32)
+        ktx[o, 1, 0] = total.astype(BF16)
+        begin(out)
+
+    def pass_mine(o, out, inbound=None, landed=None):
+        arrive(value_sum[o])
+        dk, dv = dka[o, 0, 0], dka[o, 0, 1] + vrx[o].astype(F32)
+        if inbound is not None:
+            arrive(inbound)
+            dk, dv = dk + landed[0, 0].astype(F32), dv + landed[0, 1].astype(F32)
+        ktx[o, 0, 0] = dk.astype(BF16)
+        ktx[o, 0, 1] = dv.astype(BF16)
+        begin(out)
 
     def after(t):
         @pl.when(t == 7)
         def _():
-            ktx[4] = dka[4].astype(BF16)
-            begin(*up_sum[4], *down_sum[4])
+            start_values(4)
+            pass_other(4, down_other[4])
+
+        @pl.when(t == 8)
+        def _():
+            pass_mine(4, up_mine[4])
 
         @pl.when(t == 9)
         def _():
-            ktx[3, 1] = dka[3, 1].astype(BF16)
-            begin(up_sum[3][1])
-            arrive(*up_sum[4])
-            ktx[3, 0] = (dka[3, 0] + kup[3, 0].astype(F32)).astype(BF16)
-            begin(up_sum[3][0])
+            start_values(3)
+            pass_other(3, up_other[3])
+
+        @pl.when(t == 10)
+        def _():
+            pass_mine(3, up_mine[3], up_mine[4], kup.at[3])
 
         @pl.when(t == 11)
         def _():
-            ktx[5, 0] = dka[5, 0].astype(BF16)
-            begin(down_sum[3][0])
-            arrive(*down_sum[4])
-            ktx[5, 1] = (dka[5, 1] + kdn[3, 1].astype(F32)).astype(BF16)
-            begin(down_sum[3][1])
-
-        for hop in (2, 1):
-            @pl.when(t == 14 - hop)
-            def _():
-                for j in range(2):
-                    arrive(up_sum[hop + 1][1 - j])
-                    ktx[hop, 1 - j] = (dka[hop, 1 - j] + kup[hop, 1 - j].astype(F32)).astype(BF16)
-                    begin(up_sum[hop][1 - j])
-                    arrive(down_sum[hop + 1][j])
-                    ktx[8 - hop, j] = (dka[8 - hop, j] + kdn[hop, j].astype(F32)).astype(BF16)
-                    begin(down_sum[hop][j])
+            start_values(5)
+            pass_other(5, down_other[3], down_other[4], kdn.at[3])
+
+        @pl.when(t == 12)
+        def _():
+            start_values(2)
+            start_values(6)
+            pass_mine(5, down_mine[3])
+            pass_other(2, up_other[2], up_other[3], kup.at[2])
+            pass_other(6, down_other[2], down_other[3], kdn.at[2])
+
+        @pl.when(t == 13)
+        def _():
+            start_values(1)
+            start_values(7)
+            pass_mine(2, up_mine[2], up_mine[3], kup.at[2])
+            pass_other(1, up_other[1], up_other[2], kup.at[1])
+            pass_other(7, down_other[1], down_other[2], kdn.at[1])
+            pass_mine(6, down_mine[2], down_mine[3], kdn.at[2])
 
         @pl.when(t == 14)
         def _():
             qtx[OPP] = dqa[OPP].astype(BF16)
             begin(*opp_sum)
+            pass_mine(1, up_mine[1], up_mine[2], kup.at[1])
+            pass_mine(7, down_mine[1], down_mine[2], kdn.at[1])
 
     def both(t, carry):
         packed = jnp.int32(0)
@@ -414,15 +465,16 @@
     qtx[RIGHT, 0] = (dqa[RIGHT, 0] + orx[0].astype(F32)).astype(BF16)
     qtx[LEFT, 1] = (dqa[LEFT, 1] + orx[1].astype(F32)).astype(BF16)
     begin(right_sum[1], left_sum[1])
-    arrive(up_sum[1][1], down_sum[1][1])
-    ytx[...] = (dka[0, 1] + kup[0, 1].astype(F32) + kdn[0, 1].astype(F32)).astype(BF16)
+    start_values(0)
+    arrive(up_other[1], down_other[1])
+    ktx[0, 1, 0] = (dka[0, 1, 0] + kup[0, 1, 0].astype(F32) + kdn[0, 1, 0].astype(F32)).astype(BF16)
     begin(across_sum)
-    arrive(up_sum[1][0], down_sum[1][0])
-    total = dka[0, 0] + kup[0, 0].astype(F32) + kdn[0, 0].astype(F32)
-    arrive(across_sum)
-    total = total + yrx[...].astype(F32)
-    dk_out[...] = total[0] * SCALE
-    dv_out[...] = total[1]
+    arrive(up_mine[1], down_mine[1])
+    dk = dka[0, 0, 0] + kup[0, 0, 0].astype(F32) + kdn[0, 0, 0].astype(F32)
+    dv = dka[0, 0, 1] + kup[0, 0, 1].astype(F32) + kdn[0, 0, 1].astype(F32)
+    arrive(value_sum[0], across_sum)
+    dk_out[...] = (dk + yrx[...].astype(F32)) * SCALE
+    dv_out[...] = dv + vrx[0].astype(F32)
     for j, (a, b) in enumerate(((1, 0), (0, 1))):
         arrive(right_sum[a], left_sum[b])
         dq = dqa[OWN, j] + qrx[0, j].astype(F32) + qrx[1, j].astype(F32)
@@ -430,14 +482,17 @@
 
     for copy in to_right + to_left + far_right + far_left + [across, across_sum]:
         copy.wait_send()
-    for group in up_kv + down_kv + list(up_sum.values()) + list(down_sum.values()):
+    for group in up_kv + down_kv:
         for copy in group:
+            copy.wait_send()
+    for group in (values, up_mine, up_other, down_mine, down_other, value_sum):
+        for copy in group.values():
             copy.wait_send()
     for copy in opp_sum + right_sum + left_sum:
         copy.wait_send()
 
 
-N_COPIES = 3 + 3 + 2 + 2 + 1 + 7 + 7 + 7 + 7 + 1 + 2 + 2 + 2
+N_COPIES = 16 + 22 + 23
 
 
 def grads(fold, order, q, do, out, lse, k, v):
@@ -466,8 +521,8 @@
             pltpu.VMEM((NZ, NY, 2, TOK, BLK), BF16),
             pltpu.VMEM((4, NY, 2, TOK, BLK), BF16),
             pltpu.VMEM((4, NY, 2, TOK, BLK), BF16),
-            pltpu.VMEM((2, TOK, BLK), BF16),
-            pltpu.VMEM((2, TOK, BLK), BF16),
+            pltpu.VMEM((NZ, TOK, BLK), BF16),
+            pltpu.VMEM((TOK, BLK), BF16),
             pltpu.VMEM((4, 2, BLK, ROWS), BF16),
             pltpu.VMEM((2, 2, BLK, ROWS), BF16),
             pltpu.VMEM((2, BLK, ROWS), BF16),

time: 86.1 us -> 85.5 us (level)
  no operation moved by 1% of the time
where the time goes in v5:
time: 85.5 us; the launch traced here: 85.4 us
  Pallas kernels  79.9 us (93%)
  local copies, waits for them, and re-layouts  3.34 us (4%)
  between operations  1.97 us (2%)
    pallas_call x1, Pallas kernels, grads(): pl.pallas_call(functools.partial(kernel, fold), out_shape=(jax.ShapeDtype...  79.9 us
    unnamed x7, local copies, waits for them, and re-layouts  2.76 us

profile of v5, /device:TPU:16, one launch (start us, length us, event | category | flops | bytes accessed | tf_op | source)
XLA Modules:
  0.0 85.4 jit_solution(5788704518418536093)
XLA Ops:
  0.6 0.0 copy-start.1
  0.6 0.6 copy-done.1
  1.3 0.6 fusion
  1.9 0.0 copy-start
  3.2 0.0 copy-done
  3.2 80.1 %conditional.1 = ((f32[2,512,128]{2,1,0:T(8,128)S(1)}, f32[256,128]{1,0:T(8,128)S(1)}, f32[256,128]{1,0:T(8,128)S(1)})) conditional(s32[]{:T(128)} %bitcast, (s32[128]{0:T(128)S(1)}, bf16[2,512,128]{2,1,0:T(8,128)(2,1)}, bf16[2,512,128]{2,1,0:T(8,128)(2,1)}, bf16[2,512,128]{2,1,0:T(8,128)(2,1)}, f32[4,256]{1,0:T(4,128)S(1)}, ...), branch_computations={%region_0.0_spmd, %region_1.0_spmd} | conditional | bytes 8 | solution.py:553
  3.2 79.9 %whole.1 = (f32[2,512,128]{2,1,0:T(8,128)S(1)}, f32[256,128]{1,0:T(8,128)S(1)}, f32[256,128]{1,0:T(8,128)S(1)}) custom-call(s32[128]{0:T(128)S(1)} %get-tuple-element.37.order, bf16[2,512,128]{2,1,0:T(8,128)(2,1)} %get-tuple-element.38.q_in, bf16[2,512,128]{2,1,0:T(8,128)(2,1)} %get-tuple-element.39.do_in, bf16[2,512,128]{2,1,0:T(8,128)(2,1)} %get-tuple-element.40.out_in, ...), custom_call_target="tpu_custom_call" | custom-call | tf_op jit(solution)/shard_map/cond/branch_0_fun/whole/pallas_call | solution.py:507
  83.3 0.8 copy.19
  84.1 0.7 copy.20
  84.7 0.7 copy.21
Async XLA Ops:
  0.6 0.7 copy-start.1
  1.9 1.3 %copy-start = (f32[256,4]{0,1:T(4,128)S(1)}, f32[256,4]{0,1:T(4,128)}, u32[]{:S(2)}) copy-start(f32[256,4]{0,1:T(4,128)} %param.13) | copy-start | bytes 12292

commit v6 on v5

--- a/solution.py
+++ b/solution.py
@@ -200,13 +200,12 @@
         owner = x * (NY * NZ) + (y + j) % NY * NZ + (z + o) % NZ
         return order[2 * ((x + i) % NX * (NY * NZ) + plane)], order[2 * owner]
 
-    def folded(i, o, parts):
-        size = BLK * len(parts)
+    def folded(i, parts):
         state = {"p": [], "ds": [], "dsb": []}
         chunks = []
 
         def stack(index):
-            return lambda: jnp.concatenate([kv[o, j, index, :BLK] for j in parts], axis=0)
+            return lambda: jnp.concatenate([kv[o, j, index, :BLK] for o, j in parts], axis=0)
 
         def end_later(made, h):
             state["p"].append(made[0])
@@ -216,7 +215,7 @@
                 ds = jnp.concatenate(state["ds"], axis=1)
                 state["dv"] = dot(p, qn[i, 1, 1])
                 state["dk"] = dot(ds, qn[i, 1, 0])
-                state["dq"] = dot(jnp.concatenate([kt[o, j, :, :BLK] for j in parts], axis=1), ds)
+                state["dq"] = dot(jnp.concatenate([kt[o, j, :, :BLK] for o, j in parts], axis=1), ds)
 
         for h in range(2):
             chunks.append(
@@ -227,17 +226,17 @@
             )
 
         weights = []
-        for n, j in enumerate(parts):
+        for n, (o, j) in enumerate(parts):
             query_first, key_first = first_block(i, o, j)
             later = query_first < key_first
             slot = later.astype(jnp.int32)
             weight = later.astype(F32)
             weights.append(weight)
 
-            def pick(index, later=later, j=j):
+            def pick(index, later=later, o=o, j=j):
                 return lambda: lax.select(later, kv[o, j, index, BLK:], kv[o, j, index, :BLK])
 
-            def end_same(made, n=n, j=j, slot=slot, weight=weight, later=later):
+            def end_same(made, n=n, o=o, j=j, slot=slot, weight=weight):
                 p, ds = made
                 dv, dk = dot(p, qn[i, slot, 1]), dot(ds, qn[i, slot, 0])
                 rows = slice(n * BLK, n * BLK + BLK)
@@ -249,9 +248,9 @@
                 state["dsb"].append(ds)
                 if n == len(parts) - 1:
                     turned = []
-                    for m, (jm, wm) in enumerate(zip(parts, weights)):
-                        late = kt[o, jm, :, BLK:] * wm.astype(BF16)
-                        early = kt[o, jm, :, :BLK] * (1.0 - wm).astype(BF16)
+                    for (om, jm), wm in zip(parts, weights):
+                        late = kt[om, jm, :, BLK:] * wm.astype(BF16)
+                        early = kt[om, jm, :, :BLK] * (1.0 - wm).astype(BF16)
                         turned.append(jnp.concatenate([late, early], axis=0))
                     both = dot(jnp.concatenate(turned, axis=1), jnp.concatenate(state["dsb"], axis=0))
                     dqa[i, 1] += state["dq"] + both[:BLK]
@@ -266,15 +265,15 @@
             )
         return chunks
 
-    def whole(i, o, parts):
+    def whole(i, parts):
         hidden = []
-        for j in parts:
+        for o, j in parts:
             query_first, key_first = first_block(i, o, j)
             hidden.append(jnp.where(query_first > key_first, 0.0, 1e30).astype(F32))
         chunks = []
 
         def stack(index):
-            return lambda: jnp.concatenate([kv[o, j, index] for j in parts], axis=0)
+            return lambda: jnp.concatenate([kv[o, j, index] for o, j in parts], axis=0)
 
         for slot in range(2):
             state = {"p": [], "ds": []}
@@ -288,11 +287,11 @@
                     state["p"].append(made[0])
                     state["ds"].append(made[1])
                     cut = slice(h * TOK, h * TOK + TOK)
-                    dqa[i, slot, :, cut] += dot(jnp.concatenate([kt[o, j] for j in parts], axis=1), made[1])
+                    dqa[i, slot, :, cut] += dot(jnp.concatenate([kt[o, j] for o, j in parts], axis=1), made[1])
                     if h == 1:
                         dv = dot(jnp.concatenate(state["p"], axis=1), qn[i, slot, 1])
                         dk = dot(jnp.concatenate(state["ds"], axis=1), qn[i, slot, 0])
-                        for n, j in enumerate(parts):
+                        for n, (o, j) in enumerate(parts):
                             dka[o, j, 0] += dk[n * TOK : n * TOK + TOK]
                             dka[o, j, 1] += dv[n * TOK : n * TOK + TOK]
 
@@ -302,7 +301,10 @@
     step = folded if fold else whole
 
     def work(*steps):
-        pipelined([c for i, o, parts in steps for c in step(i, o, parts)])
+        pipelined([c for i, parts in steps for c in step(i, parts)])
+
+    def both_y(o):
+        return [(o, 0), (o, 1)]
 
     pipelined(own_chunks())
 
@@ -311,25 +313,29 @@
     arrive(up_kv[0][0], down_kv[0][0])
     begin(up_kv[1][0], down_kv[1][0], values[7], values[1])
     kt[0, 1] = kv[0, 1, 0].T
-    work((OWN, 0, (1,)))
+    work((OWN, [(0, 1)]))
+
+    def neighbours(j, carry):
+        @pl.when(j == 1)
+        def _():
+            arrive(up_kv[0][1], down_kv[0][1])
+            begin(up_kv[1][1], down_kv[1][1])
+            arrive(values[7], values[1])
+
+        for o in (1, 7):
+            kt[o, j] = kv[o, j, 0].T
+        work((OWN, [(1, j), (7, j)]))
+        return carry
+
+    lax.fori_loop(0, 2, neighbours, jnp.int32(0))
 
     table = [
-        (OWN, 1, OWN, 7), (OWN, 2, OWN, 6),
-        (LEFT, 1, RIGHT, 1), (LEFT, 7, RIGHT, 7), (LEFT, 2, RIGHT, 2), (LEFT, 6, RIGHT, 6),
-        (OWN, 4, LEFT, 4), (RIGHT, 4, OPP, 4), (OWN, 3, LEFT, 3), (RIGHT, 3, OPP, 3), (OWN, 5, LEFT, 5), (RIGHT, 5, OPP, 5),
-        (OPP, 2, OPP, 6), (OPP, 1, OPP, 7), (OPP, 0, LEFT, 0),
+        (OWN, 2), (LEFT, 1), (RIGHT, 1), (LEFT, 2), (RIGHT, 2),
+        (OWN, 3), (LEFT, 3), (RIGHT, 3), (OPP, 3), (OPP, 2), (OPP, 1),
     ]
 
     def before(t):
         @pl.when(t == 0)
-        def _():
-            arrive(up_kv[0][1], down_kv[0][1])
-            begin(up_kv[1][1], down_kv[1][1])
-            turn_keys(1)
-            turn_keys(7)
-            arrive(values[7], values[1])
-
-        @pl.when(t == 1)
         def _():
             arrive(up_kv[1][0], down_kv[1][0])
             begin(up_kv[2][0], down_kv[2][0], values[6], values[2])
@@ -339,7 +345,7 @@
             turn_keys(6)
             arrive(values[6], values[2])
 
-        @pl.when(t == 2)
+        @pl.when(t == 1)
         def _():
             arrive(to_right[0], to_right[2], to_left[1], to_left[2])
             begin(*far_right, *far_left)
@@ -347,31 +353,40 @@
             turn_queries(LEFT, from_left, rows_left)
             turn_queries(RIGHT, from_right, rows_right)
 
-        @pl.when(t == 3)
+        @pl.when(t == 2)
         def _():
             arrive(up_kv[2][0])
             begin(up_kv[3][0], values[5])
             arrive(down_kv[2][0], down_kv[2][1])
             begin(down_kv[3][0], values[3])
 
-        @pl.when(t == 4)
+        @pl.when(t == 3)
         def _():
             arrive(up_kv[2][1])
             turn_keys(3)
             turn_keys(5)
 
-        @pl.when(t == 5)
+        @pl.when(t == 4)
         def _():
             arrive(up_kv[3][0])
             begin(values[4])
 
-        @pl.when(t == 6)
+        @pl.when(t == 5)
         def _():
             arrive(*far_right, *far_left)
             turn_queries(OPP, from_opp, rows_opp)
             arrive(down_kv[3][0])
             turn_keys(4)
-            arrive(values[3], values[5], values[4])
+            arrive(values[4])
+
+            def farthest(n, carry):
+                work((2 * n, both_y(4)), (2 * n + 1, both_y(4)))
+                return carry
+
+            lax.fori_loop(0, 2, farthest, jnp.int32(0))
+            start_values(4)
+            pass_other(4, down_other[4])
+            arrive(values[3], values[5])
 
     def start_values(o):
         ktx[o, 1, 1] = dka[o, 1, 1].astype(BF16)
@@ -396,71 +411,57 @@
         begin(out)
 
     def after(t):
-        @pl.when(t == 7)
-        def _():
-            start_values(4)
-            pass_other(4, down_other[4])
+        @pl.when(t == 5)
+        def _():
+            pass_mine(4, up_mine[4])
 
         @pl.when(t == 8)
         def _():
-            pass_mine(4, up_mine[4])
+            start_values(3)
+            start_values(5)
+            pass_other(3, up_other[3])
+            pass_other(5, down_other[3], down_other[4], kdn.at[3])
 
         @pl.when(t == 9)
-        def _():
-            start_values(3)
-            pass_other(3, up_other[3])
-
-        @pl.when(t == 10)
-        def _():
-            pass_mine(3, up_mine[3], up_mine[4], kup.at[3])
-
-        @pl.when(t == 11)
-        def _():
-            start_values(5)
-            pass_other(5, down_other[3], down_other[4], kdn.at[3])
-
-        @pl.when(t == 12)
         def _():
             start_values(2)
             start_values(6)
+            pass_mine(3, up_mine[3], up_mine[4], kup.at[3])
             pass_mine(5, down_mine[3])
             pass_other(2, up_other[2], up_other[3], kup.at[2])
             pass_other(6, down_other[2], down_other[3], kdn.at[2])
 
-        @pl.when(t == 13)
+        @pl.when(t == 10)
         def _():
             start_values(1)
             start_values(7)
             pass_mine(2, up_mine[2], up_mine[3], kup.at[2])
+            pass_mine(6, down_mine[2], down_mine[3], kdn.at[2])
             pass_other(1, up_other[1], up_other[2], kup.at[1])
             pass_other(7, down_other[1], down_other[2], kdn.at[1])
-            pass_mine(6, down_mine[2], down_mine[3], kdn.at[2])
-
-        @pl.when(t == 14)
-        def _():
-            qtx[OPP] = dqa[OPP].astype(BF16)
-            begin(*opp_sum)
-            pass_mine(1, up_mine[1], up_mine[2], kup.at[1])
-            pass_mine(7, down_mine[1], down_mine[2], kdn.at[1])
-
-    def both(t, carry):
+
+    def both_ways(t, carry):
         packed = jnp.int32(0)
-        for n, (ia, oa, ib, ob) in enumerate(table):
-            packed = jnp.where(t == n, jnp.int32(ia + 4 * oa + 32 * ib + 128 * ob), packed)
-        pl.when(t < 7)(lambda: before(t))
-        work(
-            (packed % 4, packed // 4 % 8, (0, 1)),
-            (packed // 32 % 4, packed // 128, (0, 1)),
-        )
-        pl.when(t > 6)(lambda: after(t))
+        for n, (i, distance) in enumerate(table):
+            packed = jnp.where(t == n, jnp.int32(i + 4 * distance), packed)
+        pl.when(t < 6)(lambda: before(t))
+        distance = packed // 4
+        work((packed % 4, both_y(distance) + both_y(NZ - distance)))
+        pl.when(t > 4)(lambda: after(t))
         return carry
 
-    lax.fori_loop(0, len(table), both, jnp.int32(0))
-    work((RIGHT, 0, (0, 1)))
+    lax.fori_loop(0, len(table), both_ways, jnp.int32(0))
+    work((OPP, both_y(0)), (LEFT, both_y(0)))
+    qtx[OPP] = dqa[OPP].astype(BF16)
+    begin(*opp_sum)
+    qtx[LEFT, 0] = dqa[LEFT, 0].astype(BF16)
+    begin(left_sum[0])
+    pass_mine(1, up_mine[1], up_mine[2], kup.at[1])
+    pass_mine(7, down_mine[1], down_mine[2], kdn.at[1])
+    work((RIGHT, both_y(0)))
 
     qtx[RIGHT, 1] = dqa[RIGHT, 1].astype(BF16)
-    qtx[LEFT, 0] = dqa[LEFT, 0].astype(BF16)
-    begin(right_sum[0], left_sum[0])
+    begin(right_sum[0])
     arrive(*opp_sum)
     qtx[RIGHT, 0] = (dqa[RIGHT, 0] + orx[0].astype(F32)).astype(BF16)
     qtx[LEFT, 1] = (dqa[LEFT, 1] + orx[1].astype(F32)).astype(BF16)

time: 85.5 us -> 72.5 us (0.85)
  Pallas kernels: 79.9 us -> 66.5 us
    pallas_call x1, Pallas kernels: 79.9 us -> 66.5 us  [grads(): pl.pallas_call(functools.partial(kernel, fold), out_shape=(jax.ShapeDtype...]
where the time goes in v6:
time: 72.5 us; the launch traced here: 72 us
  Pallas kernels  66.5 us (92%)
  local copies, waits for them, and re-layouts  3.34 us (5%)
  between operations  1.97 us (3%)
    pallas_call x1, Pallas kernels, grads(): pl.pallas_call(functools.partial(kernel, fold), out_shape=(jax.ShapeDtype...  66.5 us
    unnamed x7, local copies, waits for them, and re-layouts  2.76 us

profile of v6, /device:TPU:16, one launch (start us, length us, event | category | flops | bytes accessed | tf_op | source)
XLA Modules:
  0.0 72.0 jit_solution(3573745821193431213)
XLA Ops:
  0.6 0.0 copy-start.1
  0.6 0.6 copy-done.1
  1.3 0.6 fusion
  1.9 0.0 copy-start
  3.2 0.0 copy-done
  3.2 66.7 %conditional.1 = ((f32[2,512,128]{2,1,0:T(8,128)S(1)}, f32[256,128]{1,0:T(8,128)S(1)}, f32[256,128]{1,0:T(8,128)S(1)})) conditional(s32[]{:T(128)} %bitcast, (s32[128]{0:T(128)S(1)}, bf16[2,512,128]{2,1,0:T(8,128)(2,1)}, bf16[2,512,128]{2,1,0:T(8,128)(2,1)}, bf16[2,512,128]{2,1,0:T(8,128)(2,1)}, f32[4,256]{1,0:T(4,128)S(1)}, ...), branch_computations={%region_0.0_spmd, %region_1.0_spmd} | conditional | bytes 8 | solution.py:554
  3.4 66.5 %folded.1 = (f32[2,512,128]{2,1,0:T(8,128)S(1)}, f32[256,128]{1,0:T(8,128)S(1)}, f32[256,128]{1,0:T(8,128)S(1)}) custom-call(s32[128]{0:T(128)S(1)} %get-tuple-element.47.order, bf16[2,512,128]{2,1,0:T(8,128)(2,1)} %get-tuple-element.48.q_in, bf16[2,512,128]{2,1,0:T(8,128)(2,1)} %get-tuple-element.49.do_in, bf16[2,512,128]{2,1,0:T(8,128)(2,1)} %get-tuple-element.50.out_in, ...), custom_call_target="tpu_custom_call" | custom-call | tf_op jit(solution)/shard_map/cond/branch_1_fun/folded/pallas_call | solution.py:508
  69.9 0.8 %copy.19 = f32[256,4,128]{2,1,0:T(4,128)} copy(f32[256,4,128]{2,1,0:T(4,128)S(1)} %bitcast.16) | data formatting | bytes 1048576
  70.7 0.7 copy.20
  71.4 0.7 copy.21
Async XLA Ops:
  0.6 0.7 copy-start.1
  1.9 1.3 %copy-start = (f32[256,4]{0,1:T(4,128)S(1)}, f32[256,4]{0,1:T(4,128)}, u32[]{:S(2)}) copy-start(f32[256,4]{0,1:T(4,128)} %param.13) | copy-start | bytes 12292

commit v7 on v6

--- a/solution.py
+++ b/solution.py
@@ -85,15 +85,24 @@
     to_left += [send(rw.at[OWN], rows_right, left)]
     far_right = [send(from_left.at[0], from_opp.at[0], right), send(rows_left.at[0], rows_opp.at[0], right)]
     far_left = [send(from_right.at[1], from_opp.at[1], left), send(rows_right.at[1], rows_opp.at[1], left)]
-    across = send(kv.at[0, 0], kv.at[0, 1], partner)
+    across = [send(k_in, kv.at[0, 1, 0], partner), send(v_in, kv.at[0, 1, 1], partner)]
+    own_up = [send(k_in, kv.at[7, 0, 0], up), send(v_in, kv.at[7, 0, 1], up)]
+    own_down = [send(k_in, kv.at[1, 0, 0], down), send(v_in, kv.at[1, 0, 1], down)]
     values = {o: send(kv.at[o, 0, 1], kv.at[o, 1, 1], partner) for o in range(1, NZ)}
     up_kv = [
-        [send(kv.at[-s % NZ, 0], kv.at[7 - s, 0], up), send(kv.at[-s % NZ, 1, 0], kv.at[7 - s, 1, 0], up)]
+        [
+            send(kv.at[-s % NZ, 0], kv.at[7 - s, 0], up) if s else None,
+            send(kv.at[-s % NZ, 1, 0], kv.at[7 - s, 1, 0], up),
+        ]
         for s in range(3)
     ]
     up_kv += [[send(kv.at[5, 0], kv.at[4, 0], up)]]
     down_kv = [
-        [send(kv.at[s, 0], kv.at[s + 1, 0], down), send(kv.at[s, 1, 0], kv.at[s + 1, 1, 0], down)] for s in range(3)
+        [
+            send(kv.at[s, 0], kv.at[s + 1, 0], down) if s else None,
+            send(kv.at[s, 1, 0], kv.at[s + 1, 1, 0], down),
+        ]
+        for s in range(3)
     ]
     down_kv += [[send(kv.at[3, 1, 0], kv.at[4, 1, 0], down)]]
     up_mine = {o: send(ktx.at[o, 0], kup.at[o - 1, 0], up) for o in (4, 3, 2, 1)}
@@ -126,10 +135,8 @@
     ]
     own = [pltpu.make_async_copy(src, dst, osem.at[n]) for n, (src, dst) in enumerate(own)]
     begin(*own)
-    own[0].wait()
-    own[1].wait()
     pl.semaphore_wait(barrier, 5)
-    begin(across, up_kv[0][0], down_kv[0][0])
+    begin(across[0], own_up[0], own_down[0], across[1], own_up[1], own_down[1])
     own[2].wait()
     own[3].wait()
     begin(to_left[1], to_right[1])
@@ -137,6 +144,8 @@
     own[5].wait()
     begin(to_right[0], to_left[0])
 
+    own[0].wait()
+    own[1].wait()
     own[6].wait()
     own[7].wait()
     for j in range(2):
@@ -265,7 +274,7 @@
             )
         return chunks
 
-    def whole(i, parts):
+    def whole(i, parts, slots=(0, 1)):
         hidden = []
         for o, j in parts:
             query_first, key_first = first_block(i, o, j)
@@ -275,7 +284,7 @@
         def stack(index):
             return lambda: jnp.concatenate([kv[o, j, index] for o, j in parts], axis=0)
 
-        for slot in range(2):
+        for slot in slots:
             state = {"p": [], "ds": []}
             for h in range(2):
                 lse2 = row(i, slot, 0, h)
@@ -301,51 +310,53 @@
     step = folded if fold else whole
 
     def work(*steps):
-        pipelined([c for i, parts in steps for c in step(i, parts)])
+        pipelined([c for at in steps for c in step(*at)])
 
     def both_y(o):
         return [(o, 0), (o, 1)]
 
     pipelined(own_chunks())
 
-    arrive(across)
+    arrive(*across)
     begin(up_kv[0][1], down_kv[0][1])
-    arrive(up_kv[0][0], down_kv[0][0])
+    arrive(*own_up, *own_down)
     begin(up_kv[1][0], down_kv[1][0], values[7], values[1])
     kt[0, 1] = kv[0, 1, 0].T
     work((OWN, [(0, 1)]))
 
-    def neighbours(j, carry):
-        @pl.when(j == 1)
+    def neighbours(n, carry):
+        @pl.when(n == 1)
         def _():
             arrive(up_kv[0][1], down_kv[0][1])
             begin(up_kv[1][1], down_kv[1][1])
             arrive(values[7], values[1])
 
-        for o in (1, 7):
+        @pl.when(n == 2)
+        def _():
+            arrive(up_kv[1][0], down_kv[1][0])
+            begin(up_kv[2][0], down_kv[2][0], values[6], values[2])
+
+        @pl.when(n == 3)
+        def _():
+            arrive(up_kv[1][1], down_kv[1][1])
+            begin(up_kv[2][1], down_kv[2][1])
+            arrive(values[6], values[2])
+
+        distance, j = 1 + n // 2, n % 2
+        for o in (distance, NZ - distance):
             kt[o, j] = kv[o, j, 0].T
-        work((OWN, [(1, j), (7, j)]))
+        work((OWN, [(distance, j), (NZ - distance, j)]))
         return carry
 
-    lax.fori_loop(0, 2, neighbours, jnp.int32(0))
+    lax.fori_loop(0, 4, neighbours, jnp.int32(0))
 
     table = [
-        (OWN, 2), (LEFT, 1), (RIGHT, 1), (LEFT, 2), (RIGHT, 2),
+        (LEFT, 1), (RIGHT, 1), (LEFT, 2), (RIGHT, 2),
         (OWN, 3), (LEFT, 3), (RIGHT, 3), (OPP, 3), (OPP, 2), (OPP, 1),
     ]
 
     def before(t):
         @pl.when(t == 0)
-        def _():
-            arrive(up_kv[1][0], down_kv[1][0])
-            begin(up_kv[2][0], down_kv[2][0], values[6], values[2])
-            arrive(up_kv[1][1], down_kv[1][1])
-            begin(up_kv[2][1], down_kv[2][1])
-            turn_keys(2)
-            turn_keys(6)
-            arrive(values[6], values[2])
-
-        @pl.when(t == 1)
         def _():
             arrive(to_right[0], to_right[2], to_left[1], to_left[2])
             begin(*far_right, *far_left)
@@ -353,25 +364,25 @@
             turn_queries(LEFT, from_left, rows_left)
             turn_queries(RIGHT, from_right, rows_right)
 
-        @pl.when(t == 2)
+        @pl.when(t == 1)
         def _():
             arrive(up_kv[2][0])
             begin(up_kv[3][0], values[5])
             arrive(down_kv[2][0], down_kv[2][1])
             begin(down_kv[3][0], values[3])
 
-        @pl.when(t == 3)
+        @pl.when(t == 2)
         def _():
             arrive(up_kv[2][1])
             turn_keys(3)
             turn_keys(5)
 
-        @pl.when(t == 4)
+        @pl.when(t == 3)
         def _():
             arrive(up_kv[3][0])
             begin(values[4])
 
-        @pl.when(t == 5)
+        @pl.when(t == 4)
         def _():
             arrive(*far_right, *far_left)
             turn_queries(OPP, from_opp, rows_opp)
@@ -411,18 +422,18 @@
         begin(out)
 
     def after(t):
-        @pl.when(t == 5)
+        @pl.when(t == 4)
         def _():
             pass_mine(4, up_mine[4])
 
-        @pl.when(t == 8)
+        @pl.when(t == 7)
         def _():
             start_values(3)
             start_values(5)
             pass_other(3, up_other[3])
             pass_other(5, down_other[3], down_other[4], kdn.at[3])
 
-        @pl.when(t == 9)
+        @pl.when(t == 8)
         def _():
             start_values(2)
             start_values(6)
@@ -431,7 +442,7 @@
             pass_other(2, up_other[2], up_other[3], kup.at[2])
             pass_other(6, down_other[2], down_other[3], kdn.at[2])
 
-        @pl.when(t == 10)
+        @pl.when(t == 9)
         def _():
             start_values(1)
             start_values(7)
@@ -444,28 +455,40 @@
         packed = jnp.int32(0)
         for n, (i, distance) in enumerate(table):
             packed = jnp.where(t == n, jnp.int32(i + 4 * distance), packed)
-        pl.when(t < 6)(lambda: before(t))
+        pl.when(t < 5)(lambda: before(t))
+
+        @pl.when(t == 9)
+        def _():
+            work((OPP, both_y(0)))
+
         distance = packed // 4
         work((packed % 4, both_y(distance) + both_y(NZ - distance)))
-        pl.when(t > 4)(lambda: after(t))
+        pl.when(t > 3)(lambda: after(t))
         return carry
 
     lax.fori_loop(0, len(table), both_ways, jnp.int32(0))
-    work((OPP, both_y(0)), (LEFT, both_y(0)))
     qtx[OPP] = dqa[OPP].astype(BF16)
     begin(*opp_sum)
+    if fold:
+        work((LEFT, both_y(0)))
+    else:
+        work((LEFT, both_y(0), (0,)), (RIGHT, both_y(0), (1,)))
+        qtx[RIGHT, 1] = dqa[RIGHT, 1].astype(BF16)
+        begin(right_sum[0])
     qtx[LEFT, 0] = dqa[LEFT, 0].astype(BF16)
     begin(left_sum[0])
-    pass_mine(1, up_mine[1], up_mine[2], kup.at[1])
-    pass_mine(7, down_mine[1], down_mine[2], kdn.at[1])
-    work((RIGHT, both_y(0)))
-
-    qtx[RIGHT, 1] = dqa[RIGHT, 1].astype(BF16)
-    begin(right_sum[0])
+    if fold:
+        work((RIGHT, both_y(0)))
+        qtx[RIGHT, 1] = dqa[RIGHT, 1].astype(BF16)
+        begin(right_sum[0])
+    else:
+        work((LEFT, both_y(0), (1,)), (RIGHT, both_y(0), (0,)))
     arrive(*opp_sum)
     qtx[RIGHT, 0] = (dqa[RIGHT, 0] + orx[0].astype(F32)).astype(BF16)
     qtx[LEFT, 1] = (dqa[LEFT, 1] + orx[1].astype(F32)).astype(BF16)
     begin(right_sum[1], left_sum[1])
+    pass_mine(1, up_mine[1], up_mine[2], kup.at[1])
+    pass_mine(7, down_mine[1], down_mine[2], kdn.at[1])
     start_values(0)
     arrive(up_other[1], down_other[1])
     ktx[0, 1, 0] = (dka[0, 1, 0] + kup[0, 1, 0].astype(F32) + kdn[0, 1, 0].astype(F32)).astype(BF16)
@@ -481,11 +504,12 @@
         dq = dqa[OWN, j] + qrx[0, j].astype(F32) + qrx[1, j].astype(F32)
         dq_out[j] = dq.T * SCALE
 
-    for copy in to_right + to_left + far_right + far_left + [across, across_sum]:
+    for copy in to_right + to_left + far_right + far_left + across + own_up + own_down + [across_sum]:
         copy.wait_send()
     for group in up_kv + down_kv:
         for copy in group:
-            copy.wait_send()
+            if copy is not None:
+                copy.wait_send()
     for group in (values, up_mine, up_other, down_mine, down_other, value_sum):
         for copy in group.values():
             copy.wait_send()
@@ -493,7 +517,7 @@
         copy.wait_send()
 
 
-N_COPIES = 16 + 22 + 23
+N_COPIES = 16 + 25 + 23
 
 
 def grads(fold, order, q, do, out, lse, k, v):
@@ -550,7 +574,8 @@
         key_proj.reshape(TOK, BLK),
         value.reshape(TOK, BLK),
     )
-    is_folded = block_order[0] + block_order[1] == 2 * NX * NY * NZ - 1
+    slots = jnp.arange(block_order.shape[0], dtype=jnp.int32)
+    is_folded = jnp.sum(jnp.where(slots < 2, block_order, 0)) == 2 * NX * NY * NZ - 1
     dq, dk, dv = lax.cond(is_folded, functools.partial(grads, True), functools.partial(grads, False), *args)
     return dq.reshape(query.shape), dk.reshape(key_proj.shape), dv.reshape(value.shape)
 

time: 72.5 us -> 71.3 us (0.983)
  Pallas kernels: 66.5 us -> 64.8 us
  other arithmetic: 0 us -> 1.29 us
    pallas_call x1, Pallas kernels: 66.5 us -> 64.8 us  [grads(): pl.pallas_call(functools.partial(kernel, fold), out_shape=(jax.ShapeDtype...]
    reduce_sum x0 -> x1, other arithmetic: none -> 1.29 us  [per_device(): jnp.sum(jnp.where(slots < 2, block_order, 0)) == 2 * NX * NY * NZ - 1]
where the time goes in v7:
time: 71.3 us; the launch traced here: 70.2 us
  Pallas kernels  64.8 us (91%)
  local copies, waits for them, and re-layouts  2.78 us (4%)
  between operations  1.31 us (2%)
  other arithmetic  1.29 us (2%)
    pallas_call x1, Pallas kernels, grads(): pl.pallas_call(functools.partial(kernel, fold), out_shape=(jax.ShapeDtype...  64.8 us
    unnamed x7, local copies, waits for them, and re-layouts  2.78 us

profile of v7, /device:TPU:16, one launch (start us, length us, event | category | flops | bytes accessed | tf_op | source)
XLA Modules:
  0.0 70.2 jit_solution(3764752981523521809)
XLA Ops:
  0.6 1.3 %fusion = s32[]{:T(128)} fusion(s32[128]{0:T(128)} %param.15), kind=kLoop, calls=%fused_computation.1 | loop fusion | flops 383 | bytes 516 | tf_op jit(solution)/shard_map/reduce_sum | solution.py:578
  2.6 0.0 copy-start
  2.6 0.0 copy-start.1
  2.6 0.7 copy-done
  3.3 0.0 copy-done.1
  3.3 64.8 %conditional.1 = ((f32[2,512,128]{2,1,0:T(8,128)S(1)}, f32[256,128]{1,0:T(8,128)S(1)}, f32[256,128]{1,0:T(8,128)S(1)})) conditional(s32[]{:T(128)} %convert_element_type.3, (s32[128]{0:T(128)S(1)}, bf16[2,512,128]{2,1,0:T(8,128)(2,1)}, bf16[2,512,128]{2,1,0:T(8,128)(2,1)}, bf16[2,512,128]{2,1,0:T(8,128)(2,1)}, f32[4,256]{1,0:T(4,128)S(1)}, ...), branch_computations={%region_1.2_spmd, %region_2.3_spmd} | conditional | bytes 8 | solution.py:579
  3.3 64.8 %folded.1 = (f32[2,512,128]{2,1,0:T(8,128)S(1)}, f32[256,128]{1,0:T(8,128)S(1)}, f32[256,128]{1,0:T(8,128)S(1)}) custom-call(s32[128]{0:T(128)S(1)} %get-tuple-element.47.order, bf16[2,512,128]{2,1,0:T(8,128)(2,1)} %get-tuple-element.48.q_in, bf16[2,512,128]{2,1,0:T(8,128)(2,1)} %get-tuple-element.49.do_in, bf16[2,512,128]{2,1,0:T(8,128)(2,1)} %get-tuple-element.50.out_in, ...), custom_call_target="tpu_custom_call" | custom-call | tf_op jit(solution)/shard_map/cond/branch_1_fun/folded/pallas_call | solution.py:532
  68.1 0.8 %copy.19 = f32[256,4,128]{2,1,0:T(4,128)} copy(f32[256,4,128]{2,1,0:T(4,128)S(1)} %bitcast.15) | data formatting | bytes 1048576
  68.9 0.7 copy.20
  69.5 0.7 copy.21
Async XLA Ops:
  2.6 0.7 copy-start
  2.6 0.7 copy-start.1

commit v8 on v7

--- a/solution.py
+++ b/solution.py
@@ -351,8 +351,8 @@
     lax.fori_loop(0, 4, neighbours, jnp.int32(0))
 
     table = [
-        (LEFT, 1), (RIGHT, 1), (LEFT, 2), (RIGHT, 2),
-        (OWN, 3), (LEFT, 3), (RIGHT, 3), (OPP, 3), (OPP, 2), (OPP, 1),
+        (LEFT, 2), (RIGHT, 2), (LEFT, 1), (OWN, 3),
+        (LEFT, 3), (RIGHT, 3), (OPP, 3), (OPP, 2), (RIGHT, 1), (OPP, 1),
     ]
 
     def before(t):
@@ -381,6 +381,7 @@
         def _():
             arrive(up_kv[3][0])
             begin(values[4])
+            arrive(values[3], values[5])
 
         @pl.when(t == 4)
         def _():
@@ -397,7 +398,6 @@
             lax.fori_loop(0, 2, farthest, jnp.int32(0))
             start_values(4)
             pass_other(4, down_other[4])
-            arrive(values[3], values[5])
 
     def start_values(o):
         ktx[o, 1, 1] = dka[o, 1, 1].astype(BF16)
@@ -426,14 +426,14 @@
         def _():
             pass_mine(4, up_mine[4])
 
-        @pl.when(t == 7)
+        @pl.when(t == 6)
         def _():
             start_values(3)
             start_values(5)
             pass_other(3, up_other[3])
             pass_other(5, down_other[3], down_other[4], kdn.at[3])
 
-        @pl.when(t == 8)
+        @pl.when(t == 7)
         def _():
             start_values(2)
             start_values(6)
@@ -442,12 +442,15 @@
             pass_other(2, up_other[2], up_other[3], kup.at[2])
             pass_other(6, down_other[2], down_other[3], kdn.at[2])
 
+        @pl.when(t == 8)
+        def _():
+            pass_mine(2, up_mine[2], up_mine[3], kup.at[2])
+            pass_mine(6, down_mine[2], down_mine[3], kdn.at[2])
+
         @pl.when(t == 9)
         def _():
             start_values(1)
             start_values(7)
-            pass_mine(2, up_mine[2], up_mine[3], kup.at[2])
-            pass_mine(6, down_mine[2], down_mine[3], kdn.at[2])
             pass_other(1, up_other[1], up_other[2], kup.at[1])
             pass_other(7, down_other[1], down_other[2], kdn.at[1])
 
@@ -564,6 +567,17 @@
     )(order, q, do, out, lse, k, v)
 
 
+def hand_out(dq_in, dk_in, dv_in, dq_out, dk_out, dv_out, sem):
+    copies = [
+        pltpu.make_async_copy(src, dst, sem.at[n])
+        for n, (src, dst) in enumerate(((dq_in, dq_out), (dk_in, dk_out), (dv_in, dv_out)))
+    ]
+    for copy in copies:
+        copy.start()
+    for copy in copies:
+        copy.wait()
+
+
 def per_device(query, key_proj, value, output, lse, d_output, block_order):
     args = (
         block_order,
@@ -577,6 +591,15 @@
     slots = jnp.arange(block_order.shape[0], dtype=jnp.int32)
     is_folded = jnp.sum(jnp.where(slots < 2, block_order, 0)) == 2 * NX * NY * NZ - 1
     dq, dk, dv = lax.cond(is_folded, functools.partial(grads, True), functools.partial(grads, False), *args)
+    anywhere = pl.BlockSpec(memory_space=pl.ANY)
+    dq, dk, dv = pl.pallas_call(
+        hand_out,
+        out_shape=tuple(jax.ShapeDtypeStruct(a.shape, a.dtype) for a in (dq, dk, dv)),
+        in_specs=[anywhere] * 3,
+        out_specs=(pl.BlockSpec(memory_space=pltpu.HBM),) * 3,
+        scratch_shapes=[pltpu.SemaphoreType.DMA((3,))],
+        name="hand_out",
+    )(dq, dk, dv)
     return dq.reshape(query.shape), dk.reshape(key_proj.shape), dv.reshape(value.shape)
 
 

time: 71.3 us -> 79.9 us (1.12); the launches traced: 70.2 us -> 79.7 us
  Pallas kernels: 64.8 us -> 76 us
  local copies, waits for them, and re-layouts: 2.78 us -> 0.68 us
    pallas_call x1, Pallas kernels: 64.8 us -> 75.1 us  [grads(): pl.pallas_call(functools.partial(kernel, fold), out_shape=(jax.ShapeDtype...]
    unnamed x7 -> x4, local copies, waits for them, and re-layouts: 2.78 us -> 0.68 us
    pallas_call x0 -> x1, Pallas kernels: none -> 0.9 us  [per_device(): pl.pallas_call(hand_out, out_shape=tuple((jax.ShapeDtypeStruct(a.shape, a...]
where the time goes in v8:
time: 79.9 us; the launch traced here: 79.7 us
  Pallas kernels  76 us (95%)
  between operations  1.49 us (2%)
  other arithmetic  1.29 us (2%)
    pallas_call x1, Pallas kernels, grads(): pl.pallas_call(functools.partial(kernel, fold), out_shape=(jax.ShapeDtype...  75.1 us

profile of v8, /device:TPU:16, one launch (start us, length us, event | category | flops | bytes accessed | tf_op | source)
XLA Modules:
  0.0 79.7 jit_solution(1350320189692416598)
XLA Ops:
  0.6 1.3 %fusion = s32[]{:T(128)} fusion(s32[128]{0:T(128)} %param.15), kind=kLoop, calls=%fused_computation.1 | loop fusion | flops 383 | bytes 516 | tf_op jit(solution)/shard_map/reduce_sum | solution.py:592
  2.6 0.0 copy-start
  2.6 0.0 copy-start.1
  2.6 0.7 copy-done
  3.3 0.0 copy-done.1
  3.3 75.3 %conditional.1 = ((f32[2,512,128]{2,1,0:T(8,128)S(1)}, f32[256,128]{1,0:T(8,128)S(1)}, f32[256,128]{1,0:T(8,128)S(1)})) conditional(s32[]{:T(128)} %convert_element_type.3, (s32[128]{0:T(128)S(1)}, bf16[2,512,128]{2,1,0:T(8,128)(2,1)}, bf16[2,512,128]{2,1,0:T(8,128)(2,1)}, bf16[2,512,128]{2,1,0:T(8,128)(2,1)}, f32[4,256]{1,0:T(4,128)S(1)}, ...), branch_computations={%region_1.2_spmd, %region_2.3_spmd} | conditional | bytes 8 | solution.py:593
  3.3 75.1 %whole.1 = (f32[2,512,128]{2,1,0:T(8,128)S(1)}, f32[256,128]{1,0:T(8,128)S(1)}, f32[256,128]{1,0:T(8,128)S(1)}) custom-call(s32[128]{0:T(128)S(1)} %get-tuple-element.28.order, bf16[2,512,128]{2,1,0:T(8,128)(2,1)} %get-tuple-element.29.q_in, bf16[2,512,128]{2,1,0:T(8,128)(2,1)} %get-tuple-element.30.do_in, bf16[2,512,128]{2,1,0:T(8,128)(2,1)} %get-tuple-element.31.out_in, ...), custom_call_target="tpu_custom_call" | custom-call | tf_op jit(solution)/shard_map/cond/branch_0_fun/whole/pallas_call | solution.py:535
  78.6 0.9 %hand_out.1 = (f32[2,512,128]{2,1,0:T(8,128)}, f32[256,128]{1,0:T(8,128)}, f32[256,128]{1,0:T(8,128)}) custom-call(f32[2,512,128]{2,1,0:T(8,128)S(1)} %get-tuple-element.51.dq_in, f32[256,128]{1,0:T(8,128)S(1)} %get-tuple-element.52.dk_in, f32[256,128]{1,0:T(8,128)S(1)} %get-tuple-element.53.dv_in), custom_call_target="tpu_custom_call" | custom-call | tf_op jit(solution)/shard_map/hand_out/pallas_call | solution.py:595
Async XLA Ops:
  2.6 0.7 copy-start
  2.6 0.7 copy-start.1
